TPU v7x, 32 devices: a whole 2x2x4 slice. The times are simulated.
32 devices in a mesh: nodes: 8 (over z, y), feat: 4 (over x, core).
Axes of the slice: x: 2, y: 2, z: 4, core: 2. Of those that a mesh axis runs over, the one named last changes fastest.
Arguments:
- features: bfloat16 [32768, 1024], P('nodes', 'feat'), may hold values from -6 to 6
- pair_count: int32 [8, 8], P('nodes'), may hold values from 1 to 2, as said below
- send_blocks: int32 [8, 8, 2], P('nodes'), may hold values from 0 to 31
- tile_src: int32 [256, 4], P('nodes'), may hold values from 0 to 15, as said below
- tiles: bfloat16 [256, 4, 128, 128], P('nodes'), may hold values from -0.25 to 0.25
- labels: int32 [32768], P('nodes'), may hold values from 0 to 15
- w_first: bfloat16 [1024, 1024], P('feat'), may hold values from -0.1875 to 0.1875
- b_first: float32 [1024], P('feat'), may hold values from -3 to 3
- w_second: bfloat16 [1024, 16], P('feat'), may hold values from -0.1875 to 0.1875
Outputs:
- grad_first: float32 [1024, 1024], P('feat', 'nodes')
- grad_bias: float32 [1024], P('feat')
- grad_second: float32 [1024, 16], P('feat')
Inputs may be any that keep to these rules, and one draw needn't show every extreme that they name: pair_count[p, p] is 2 for every p. `tile_src`: the 32 rows of one partition name every slot 0 to 15 at least once.
All inputs are finite; a program needn't handle non-finite values.
Results may differ from a plain program's by a relative error of at most 0.015.
The roundings to bfloat16 on the way count: a program that leaves them out, or rounds other values in their place, can miss the bound.
Values may be sent and summed in bfloat16 or wider, within the bound.
A program may use at most 128 MiB of HBM per device.

v0:
```python
import math

import jax
import jax.numpy as jnp
from jax import lax
from jax.sharding import PartitionSpec as P


def shards(features, pair_count, send_blocks, tile_src, tiles, labels, w_first, b_first, w_second):
    high = lax.Precision.HIGHEST
    rows, width = features.shape
    nblocks, per_block = tile_src.shape
    blk = tiles.shape[2]
    parts = lax.axis_size("nodes")
    slots = send_blocks.shape[2]
    grades = w_second.shape[1]
    hq = w_first.shape[1] // lax.axis_size("feat")
    owner = tile_src // slots
    slot_in = tile_src % slots
    counts = pair_count[0]
    live = slot_in < counts[owner]
    weights = tiles * live[:, :, None, None].astype(jnp.bfloat16)
    table = send_blocks[0]

    def gather_sources(received):
        flat = received.reshape(parts * slots, blk, received.shape[-1])
        return flat[tile_src]

    own_one = features.reshape(nblocks, blk, width)
    arrived = lax.all_to_all(own_one[table], "nodes", split_axis=0, concat_axis=0, tiled=True)
    summed = jnp.einsum(
        "btij,btjf->bif", weights, gather_sources(arrived), preferred_element_type=jnp.float32
    )
    agg_first = (summed + own_one).astype(jnp.bfloat16).reshape(rows, width)
    partial_pre = jnp.dot(agg_first, w_first, preferred_element_type=jnp.float32)
    pre = lax.psum_scatter(partial_pre, "feat", scatter_dimension=1, tiled=True)
    pre = pre + b_first
    hidden = jnp.maximum(pre, 0.0).astype(jnp.bfloat16)
    own_two = hidden.reshape(nblocks, blk, hq)
    arrived_two = lax.all_to_all(own_two[table], "nodes", split_axis=0, concat_axis=0, tiled=True)
    agg_second = (
        jnp.einsum(
            "btij,btjf->bif",
            weights,
            gather_sources(arrived_two),
            preferred_element_type=jnp.float32,
        )
        + own_two
    )
    partial_logits = jnp.dot(
        agg_second.reshape(rows, hq), w_second.astype(jnp.float32), precision=high
    )
    logits = lax.psum(partial_logits, "feat")
    expo = jnp.exp(logits)
    probs = expo / jnp.sum(expo, axis=1, keepdims=True)
    onehot = (labels[:, None] == jnp.arange(grades, dtype=jnp.int32)[None, :]).astype(jnp.float32)
    dlog = (probs - onehot) * (1.0 / math.sqrt(rows * parts))
    dlog_b = dlog.astype(jnp.bfloat16).reshape(nblocks, blk, grades)
    contrib = jnp.einsum("btij,bif->btjf", weights, dlog_b, preferred_element_type=jnp.float32)
    slot_hit = (
        tile_src.reshape(-1)[:, None] == jnp.arange(parts * slots, dtype=jnp.int32)[None, :]
    ).astype(jnp.float32)
    slotsum = lax.dot_general(
        slot_hit,
        contrib.reshape(nblocks * per_block, blk * grades),
        (((0,), (0,)), ((), ())),
        precision=high,
    )
    returned = lax.all_to_all(
        slotsum.reshape(parts, slots, blk, grades).astype(jnp.bfloat16),
        "nodes",
        split_axis=0,
        concat_axis=0,
        tiled=True,
    ).astype(jnp.float32)
    placing = (table.reshape(-1)[None, :] == jnp.arange(nblocks, dtype=jnp.int32)[:, None]).astype(
        jnp.float32
    )
    spread = jnp.dot(placing, returned.reshape(parts * slots, blk * grades), precision=high)
    dproj_b = (dlog + spread.reshape(rows, grades)).astype(jnp.bfloat16)
    grad_second = lax.dot_general(
        hidden, dproj_b, (((0,), (0,)), ((), ())), preferred_element_type=jnp.float32
    )
    dhid = lax.dot_general(
        dproj_b, w_second, (((1,), (1,)), ((), ())), preferred_element_type=jnp.float32
    )
    dpre = jnp.where(pre > 0, dhid, 0.0)
    grad_bias = jnp.sum(dpre, axis=0)
    grad_second, grad_bias = lax.psum((grad_second, grad_bias), "nodes")
    dpre_b = dpre.astype(jnp.bfloat16)
    grad_part = lax.dot_general(
        agg_first,
        lax.all_gather(dpre_b, "feat", axis=1, tiled=True),
        (((0,), (0,)), ((), ())),
        preferred_element_type=jnp.float32,
    )
    grad_first = lax.psum_scatter(
        grad_part.astype(jnp.bfloat16), "nodes", scatter_dimension=1, tiled=True
    ).astype(jnp.float32)
    return (grad_first, grad_bias, grad_second)


def solution(mesh):
    placed = (
        P("nodes", "feat"),
        P("nodes", None),
        P("nodes", None, None),
        P("nodes", None),
        P("nodes", None, None, None),
        P("nodes"),
        P("feat", None),
        P("feat"),
        P("feat", None),
    )
    return jax.shard_map(
        shards,
        mesh=mesh,
        in_specs=placed,
        out_specs=(P("feat", "nodes"), P("feat"), P("feat", None)),
        check_vma=False,
    )
```

profile of v0, /device:TPU:0, one launch (start us, length us, event | category | flops | bytes accessed | tf_op | source)
XLA Modules:
  0.0 446.8 jit_solution(7191290962076014837)
XLA Ops:
  8.1 3.2 gather_fusion.1
  11.3 7.3 %all-to-all-start = ((bf16[8,2,128,256]{3,2,1,0:T(8,128)(2,1)}), bf16[8,2,128,256]{3,2,1,0:T(8,128)(2,1)S(1)}, u32[]{:S(2)}, u32[]{:S(2)}) async-start(bf16[8,2,128,256]{3,2,1,0:T(8,128)(2,1)} %bitcast.3), calls=%async_computation | async-start | bytes 2097152 | tf_op jit(solution)/shard_map/all_to_all | solution.py:30
  20.6 23.7 %all-to-all-done = bf16[8,2,128,256]{3,2,1,0:T(8,128)(2,1)S(1)} async-done(((bf16[8,2,128,256]{3,2,1,0:T(8,128)(2,1)}), bf16[8,2,128,256]{3,2,1,0:T(8,128)(2,1)S(1)}, u32[]{:S(2)}, u32[]{:S(2)}) %all-to-all-start) | async-done | bytes 1048608 | tf_op jit(solution)/shard_map/all_to_all | solution.py:30
  44.3 6.5 %gather_fusion.2 = bf16[128,128,256]{2,1,0:T(8,128)(2,1)} fusion(bf16[16,128,256]{2,1,0:T(8,128)(2,1)S(1)} %bitcast.60, s32[1024]{0:T(1024)S(1)} %pad_clamp_fusion), kind=kCustom, calls=%fused_computation.2 | custom fusion | bytes 16777728 | tf_op jit(solution)/shard_map/gather | solution.py:27
  50.9 7.0 %fusion = bf16[32,128,256]{2,1,0:T(8,128)(2,1)S(1)} fusion(bf16[32,128,256]{2,1,0:T(8,128)(2,1)} %bitcast.75, bf16[32,4,128,256]{3,2,1,0:T(8,128)(2,1)} %bitcast.68, bf16[32,4,128,128]{3,2,1,0:T(8,128)(2,1)} %param.13, bf16[32,4]{1,0:T(8,128)(2,1)S(1)} %copy.58), kind=kOutput, calls=%fused_computation.8 | convolution fusion | flops 1078984704 | bytes 16777472 | tf_op jit(solution)/shard_map/btij,btjf->bif/dot_general | solution.py:31
  57.9 1.3 copy-done.5
  59.2 8.1 %fusion.27 = f32[4096,1024]{1,0:T(8,128)} fusion(bf16[4096,256]{1,0:T(8,128)(2,1)S(1)} %bitcast.66, bf16[256,1024]{1,0:T(8,128)(2,1)S(1)} %copy-done), kind=kOutput, calls=%fused_computation.54 | convolution fusion | flops 2147483648 | bytes 19398656 | tf_op jit(solution)/shard_map/dot_general | solution.py:35
  67.4 125.3 %reduce-scatter.5.cloned.1.call-done = f32[4096,256]{1,0:T(8,128)} async-done(((f32[4096,1024]{1,0:T(8,128)}), f32[4096,256]{1,0:T(8,128)}) %reduce-scatter.5.cloned.1.call-update) | async-done | bytes 4194320 | tf_op jit(solution)/shard_map/reduce_scatter | solution.py:36
  192.6 2.6 maximum_convert_fusion
  195.2 1.7 gather_fusion.3
  196.9 31.3 %all_to_all.15 = bf16[8,2,128,256]{3,2,1,0:T(8,128)(2,1)S(1)} all-to-all(bf16[8,2,128,256]{3,2,1,0:T(8,128)(2,1)} %bitcast.71), channel_id=1, replica_groups=mesh['nodes'=8,'feat'=4] {'nodes'}, dimensions={0} | all-to-all | bytes 2097152 | tf_op jit(solution)/shard_map/all_to_all | solution.py:40
  228.2 6.5 %gather_fusion.4 = bf16[128,128,256]{2,1,0:T(8,128)(2,1)} fusion(bf16[16,128,256]{2,1,0:T(8,128)(2,1)S(1)} %bitcast.61, s32[1024]{0:T(1024)S(1)} %pad_clamp_fusion), kind=kCustom, calls=%fused_computation.4 | custom fusion | bytes 16777728 | tf_op jit(solution)/shard_map/gather | solution.py:27
  234.7 7.0 %bitcast_add_fusion = f32[32,128,256]{2,1,0:T(8,128)S(1)} fusion(bf16[32,128,256]{2,1,0:T(8,128)(2,1)} %bitcast.64, bf16[32,4,128,256]{3,2,1,0:T(8,128)(2,1)} %bitcast.62, bf16[32,4,128,128]{3,2,1,0:T(8,128)(2,1)} %param.13, bf16[32,4]{1,0:T(8,128)(2,1)S(1)} %copy.58), kind=kOutput, calls=%fused_computation.6 | convolution fusion | flops 1077936128 | bytes 18874624 | tf_op jit(solution)/shard_map/btij,btjf->bif/dot_general | solution.py:42
  241.7 2.7 fusion.28
  244.7 30.0 %all-reduce.3.cloned.1.call-done = f32[4096,16]{0,1:T(8,128)} async-done(((f32[4096,16]{0,1:T(8,128)}), f32[4096,16]{0,1:T(8,128)}) %all-reduce.3.cloned.1.call-update) | async-done | bytes 262160 | tf_op jit(solution)/shard_map/psum | solution.py:53
  276.8 6.9 %fusion.1 = f32[32,4,128,16]{3,2,1,0:T(8,128)} fusion(bf16[32,4,128,128]{3,2,1,0:T(8,128)(2,1)} %param.13, bf16[32,4]{1,0:T(8,128)(2,1)S(1)} %copy.58, bf16[32,128,16,1]{1,0,2,3:T(8,128)(2,1)S(1)} %bitcast.73), kind=kOutput, calls=%fused_computation.10 | convolution fusion | flops 69206016 | bytes 5374208 | tf_op jit(solution)/shard_map/btij,bif->btjf/dot_general | solution.py:59
  283.7 7.9 %reshape.98 = f32[128,2048]{1,0:T(8,128)S(1)} reshape(f32[32,4,128,16]{3,2,1,0:T(8,128)} %fusion.1) | data formatting | bytes 2097152 | tf_op jit(solution)/shard_map/reshape | solution.py:65
  293.4 5.5 %all-to-all-start.2 = ((bf16[8,2,128,16]{2,3,1,0:T(8,128)(2,1)}), bf16[8,2,128,16]{2,3,1,0:T(8,128)(2,1)S(1)}, u32[]{:S(2)}, u32[]{:S(2)}) async-start(bf16[8,2,128,16]{2,3,1,0:T(8,128)(2,1)} %copy.67), calls=%async_computation.3 | async-start | bytes 131072 | tf_op jit(solution)/shard_map/all_to_all | solution.py:69
  299.3 6.5 %all-to-all-done.2 = bf16[8,2,128,16]{2,3,1,0:T(8,128)(2,1)S(1)} async-done(((bf16[8,2,128,16]{2,3,1,0:T(8,128)(2,1)}), bf16[8,2,128,16]{2,3,1,0:T(8,128)(2,1)S(1)}, u32[]{:S(2)}, u32[]{:S(2)}) %all-to-all-start.2) | async-done | bytes 65568 | tf_op jit(solution)/shard_map/all_to_all | solution.py:69
  308.4 4.5 fusion.26
  313.0 56.1 %all-gather.2.cloned.1.call-done = bf16[4096,1024]{1,0:T(8,128)(2,1)} async-done(((bf16[4096,256]{1,0:T(8,128)(2,1)}), bf16[4096,1024]{1,0:T(8,128)(2,1)}) %all-gather.2.cloned.1.call-update) | async-done | bytes 8388624 | tf_op jit(solution)/shard_map/all_gather | solution.py:93
  369.1 6.4 %convolution_convert_fusion = bf16[256,1024]{1,0:T(8,128)(2,1)S(1)} fusion(bf16[4096,256]{1,0:T(8,128)(2,1)} %bitcast.67, bf16[4096,1024]{1,0:T(8,128)(2,1)} %all-gather.2.cloned.1.call-done), kind=kOutput, calls=%fused_computation.19 | convolution fusion | flops 2147745792 | bytes 11010048 | tf_op jit(solution)/shard_map/dot_general | solution.py:91
  376.9 37.8 %all-reduce = (f32[256]{0:T(256)}, f32[256,16]{0,1:T(8,128)}) all-reduce(f32[256]{0:T(256)S(1)} %get-tuple-element.5, f32[256,16]{0,1:T(8,128)S(1)} %fusion.29), channel_id=1, replica_groups=mesh['nodes'=8,'feat'=4] {'nodes'}, use_global_device_ids=true, to_apply=%region_5.6 | all-reduce | flops 4352 | bytes 34816 | tf_op jit(solution)/shard_map/psum | solution.py:89
  414.7 24.0 %reduce-scatter.7.cloned.1.call-done = bf16[128,256]{1,0:T(8,128)(2,1)} async-done(((bf16[1024,256]{1,0:T(8,128)(2,1)}), bf16[128,256]{1,0:T(8,128)(2,1)}) %reduce-scatter.7.cloned.1.call-update) | async-done | bytes 65552
  (68 shorter events, 13.2 us)
Async XLA Ops:
  7.2 52.0 %copy-start = (bf16[256,1024]{1,0:T(8,128)(2,1)S(1)}, bf16[256,1024]{1,0:T(8,128)(2,1)}, u32[]{:S(2)}) copy-start(bf16[256,1024]{1,0:T(8,128)(2,1)} %param.15) | copy-start | bytes 1572868
  7.2 11.4 %copy-start.9 = (s32[32,4]{0,1:T(4,128)S(1)}, s32[32,4]{0,1:T(4,128)}, u32[]{:S(2)}) copy-start(s32[32,4]{0,1:T(4,128)} %param.12) | copy-start | bytes 1540
  7.2 11.9 %copy-start.2 = (s32[1,8]{1,0:T(1,128)S(1)}, s32[1,8]{1,0:T(1,128)}, u32[]{:S(2)}) copy-start(s32[1,8]{1,0:T(1,128)} %param.10) | copy-start | bytes 100
  11.3 33.0 %all-to-all-start = ((bf16[8,2,128,256]{3,2,1,0:T(8,128)(2,1)}), bf16[8,2,128,256]{3,2,1,0:T(8,128)(2,1)S(1)}, u32[]{:S(2)}, u32[]{:S(2)}) async-start(bf16[8,2,128,256]{3,2,1,0:T(8,128)(2,1)} %bitcast.3), calls=%async_computation | async-start | bytes 2097152 | tf_op jit(solution)/shard_map/all_to_all | solution.py:30
  18.6 174.0 %reduce-scatter.5.cloned.1.call-start = ((), (), s32[]{:S(2)}) async-start(), calls=%async_computation.5 | async-start | bytes 20971520 | tf_op jit(solution)/shard_map/reduce_scatter | solution.py:36
  57.9 1.3 copy-start.5
  67.3 125.3 %copy-start.11 = (f32[256]{0:T(256)S(1)}, f32[256]{0:T(256)}, u32[]{:S(2)}) copy-start(f32[256]{0:T(256)} %param.16) | copy-start | bytes 3076
  67.3 207.4 %all-reduce.3.cloned.1.call-start = ((), (), s32[]{:S(2)}) async-start(), calls=%async_computation.6 | async-start | bytes 524288 | tf_op jit(solution)/shard_map/psum | solution.py:53
  195.2 1.7 copy-start.3
  234.7 7.0 %copy-start.8 = (bf16[256,16]{0,1:T(8,128)(2,1)S(1)}, bf16[256,16]{0,1:T(8,128)(2,1)}, u32[]{:S(2)}) copy-start(bf16[256,16]{0,1:T(8,128)(2,1)} %param.17) | copy-start | bytes 24580
  241.7 34.0 %copy-start.7 = (s32[4096]{0:T(1024)S(1)}, s32[4096]{0:T(1024)}, u32[]{:S(2)}) copy-start(s32[4096]{0:T(1024)} %param.14) | copy-start | bytes 49156
  283.7 15.5 %copy-start.10 = (s32[1,8,2]{1,2,0:T(2,128)S(1)}, s32[1,8,2]{1,2,0:T(2,128)}, u32[]{:S(2)}) copy-start(s32[1,8,2]{1,2,0:T(2,128)} %param.11) | copy-start | bytes 196
  291.9 16.4 %copy-start.6 = (f32[4096,16]{0,1:T(8,128)S(1)}, f32[4096,16]{0,1:T(8,128)}, u32[]{:S(2)}) copy-start(f32[4096,16]{0,1:T(8,128)} %all-reduce.3.cloned.1.call-done) | copy-start | bytes 786436
  293.4 12.4 %all-to-all-start.2 = ((bf16[8,2,128,16]{2,3,1,0:T(8,128)(2,1)}), bf16[8,2,128,16]{2,3,1,0:T(8,128)(2,1)S(1)}, u32[]{:S(2)}, u32[]{:S(2)}) async-start(bf16[8,2,128,16]{2,3,1,0:T(8,128)(2,1)} %copy.67), calls=%async_computation.3 | async-start | bytes 131072 | tf_op jit(solution)/shard_map/all_to_all | solution.py:69
  298.9 70.1 %all-gather.2.cloned.1.call-start = ((), (), s32[]{:S(2)}) async-start(), calls=%async_computation.7 | async-start | bytes 10485760 | tf_op jit(solution)/shard_map/all_gather | solution.py:93
  312.9 63.6 %copy-start.4 = (bf16[4096,256]{1,0:T(8,128)(2,1)S(1)}, bf16[4096,256]{1,0:T(8,128)(2,1)}, u32[]{:S(2)}) copy-start(bf16[4096,256]{1,0:T(8,128)(2,1)} %copy-done.3) | copy-start | bytes 6291460
  312.9 125.7 %reduce-scatter.7.cloned.1.call-start = ((), (), s32[]{:S(2)}) async-start(), calls=%async_computation.8 | async-start | bytes 589824
  369.0 71.2 %copy-start.1 = (bf16[256,1024]{1,0:T(8,128)(2,1)S(1)}, bf16[256,1024]{1,0:T(8,128)(2,1)}, u32[]{:S(2)}) copy-start(bf16[256,1024]{1,0:T(8,128)(2,1)} %param.15) | copy-start | bytes 1572868
Sparse Core Ops, SparseCore 0:
  67.4 125.1 reduce-scatter.4
  244.6 30.0 all-reduce.2
  313.0 55.9 all-gather.1
  376.6 61.9 reduce-scatter.6
where the time goes:
time: 447 us
  waiting for transfers between devices  266 us (60%)
  blocking collectives  69 us (15%)
  matrix products  43.9 us (10%)
  local copies, waits for them, and re-layouts  34.9 us (8%)
  between operations  14 us (3%)
  starting transfers between devices  13.2 us (3%)
  other arithmetic  6.2 us (1%)
    reduce_scatter x1, waiting for transfers between devices, shards(): pre = lax.psum_scatter(partial_pre, 'feat', scatter_dimension=1, tiled=True)  125 us
    all_gather x1, waiting for transfers between devices, shards(): lax.all_gather(dpre_b, 'feat', axis=1, tiled=True)  56.1 us
    psum x1, blocking collectives, shards(): grad_second, grad_bias = lax.psum((grad_second, grad_bias), 'nodes')  37.8 us
    all_to_all x1, blocking collectives, shards(): lax.all_to_all(own_two[table], 'nodes', split_axis=0, concat_axis=0, tile...  31.3 us
    psum x1, waiting for transfers between devices, shards(): logits = lax.psum(partial_logits, 'feat')  30 us
    unnamed x5, waiting for transfers between devices  24 us
    all_to_all x1, waiting for transfers between devices, shards(): lax.all_to_all(own_one[table], 'nodes', split_axis=0, concat_axis=0, tile...  23.7 us
    gather x2, local copies, waits for them, and re-layouts, gather_sources(): return flat[tile_src]  13.1 us
  transfers between devices with their start and end apart: 6, of which 6 were waited for; matrix products, arithmetic and copies ran while one was open for 1% of the time, Pallas kernels for 0%

commit v1 on v0

v1 whole, which is shorter than its diff:
```python
import math

import jax
import jax.numpy as jnp
from jax import lax
from jax.sharding import PartitionSpec as P


def shards(features, pair_count, send_blocks, tile_src, tiles, labels, w_first, b_first, w_second):
    high = lax.Precision.HIGHEST
    rows, width = features.shape
    nblocks, per_block = tile_src.shape
    blk = tiles.shape[2]
    parts = lax.axis_size("nodes")
    fsize = lax.axis_size("feat")
    me = lax.axis_index("feat")
    slots = send_blocks.shape[2]
    grades = w_second.shape[1]
    mine = nblocks // fsize
    mrows = rows // fsize
    live = (tile_src % slots) < pair_count[0][tile_src // slots]
    weights = tiles * live[:, :, None, None].astype(jnp.bfloat16)
    table = send_blocks[0]

    w1 = lax.all_gather(w_first, "feat", axis=0, tiled=True)
    w2 = lax.all_gather(w_second, "feat", axis=0, tiled=True)
    b1 = lax.all_gather(b_first, "feat", axis=0, tiled=True)

    own_one = features.reshape(nblocks, blk, width)
    arrived = lax.all_to_all(own_one[table], "nodes", split_axis=0, concat_axis=0, tiled=True)
    sources = arrived.reshape(parts * slots, blk, width)[tile_src]
    summed = jnp.einsum("btij,btjf->bif", weights, sources, preferred_element_type=jnp.float32)
    agg = (summed + own_one).astype(jnp.bfloat16).reshape(rows, width)
    agg = lax.all_to_all(agg, "feat", split_axis=0, concat_axis=1, tiled=True)
    pre = jnp.dot(agg, w1, preferred_element_type=jnp.float32) + b1
    hidden = jnp.maximum(pre, 0.0).astype(jnp.bfloat16)
    proj = jnp.dot(hidden, w2, preferred_element_type=jnp.float32)

    proj_part = lax.all_gather(proj, "feat", axis=0, tiled=True).reshape(nblocks, blk, grades)
    arrived_two = lax.all_to_all(proj_part[table], "nodes", split_axis=0, concat_axis=0, tiled=True)
    my_src = lax.dynamic_slice_in_dim(tile_src, me * mine, mine, 0)
    my_w = lax.dynamic_slice_in_dim(weights, me * mine, mine, 0).astype(jnp.float32)
    my_labels = lax.dynamic_slice_in_dim(labels, me * mrows, mrows, 0)
    src_two = arrived_two.reshape(parts * slots, blk, grades)[my_src]
    logits = (jnp.einsum("btij,btjf->bif", my_w, src_two, precision=high)).reshape(mrows, grades) + proj
    expo = jnp.exp(logits)
    probs = expo / jnp.sum(expo, axis=1, keepdims=True)
    onehot = (my_labels[:, None] == jnp.arange(grades, dtype=jnp.int32)[None, :]).astype(jnp.float32)
    dlog = (probs - onehot) * (1.0 / math.sqrt(rows * parts))
    dlog_b = dlog.astype(jnp.bfloat16).reshape(mine, blk, grades)
    contrib = jnp.einsum(
        "btij,bif->btjf", my_w.astype(jnp.bfloat16), dlog_b, preferred_element_type=jnp.float32
    )
    slot_hit = (
        my_src.reshape(-1)[:, None] == jnp.arange(parts * slots, dtype=jnp.int32)[None, :]
    ).astype(jnp.float32)
    slotsum = lax.dot_general(
        slot_hit,
        contrib.reshape(mine * per_block, blk * grades),
        (((0,), (0,)), ((), ())),
        precision=high,
    )
    returned = lax.all_to_all(
        slotsum.reshape(parts, slots, blk, grades), "nodes", split_axis=0, concat_axis=0, tiled=True
    )
    placing = (table.reshape(-1)[None, :] == jnp.arange(nblocks, dtype=jnp.int32)[:, None]).astype(
        jnp.float32
    )
    spread = jnp.dot(placing, returned.reshape(parts * slots, blk * grades), precision=high)
    spread = lax.psum_scatter(spread, "feat", scatter_dimension=0, tiled=True)
    dproj_b = (dlog + spread.reshape(mrows, grades)).astype(jnp.bfloat16)
    grad_second = lax.dot_general(
        hidden, dproj_b, (((0,), (0,)), ((), ())), preferred_element_type=jnp.float32
    )
    dhid = lax.dot_general(dproj_b, w2, (((1,), (1,)), ((), ())), preferred_element_type=jnp.float32)
    dpre = jnp.where(pre > 0, dhid, 0.0)
    grad_bias = jnp.sum(dpre, axis=0)
    small = jnp.concatenate([grad_second, grad_bias[:, None]], axis=1)
    small = lax.psum(small, "nodes")
    small = lax.psum_scatter(small, "feat", scatter_dimension=0, tiled=True)
    grad_part = lax.dot_general(
        agg, dpre.astype(jnp.bfloat16), (((0,), (0,)), ((), ())), preferred_element_type=jnp.float32
    ).astype(jnp.bfloat16)
    grad_part = lax.psum_scatter(grad_part, "feat", scatter_dimension=0, tiled=True)
    grad_first = lax.psum_scatter(grad_part, "nodes", scatter_dimension=1, tiled=True)
    return (grad_first.astype(jnp.float32), small[:, grades], small[:, :grades])


def solution(mesh):
    placed = (
        P("nodes", "feat"),
        P("nodes", None),
        P("nodes", None, None),
        P("nodes", None),
        P("nodes", None, None, None),
        P("nodes"),
        P("feat", None),
        P("feat"),
        P("feat", None),
    )
    return jax.shard_map(
        shards,
        mesh=mesh,
        in_specs=placed,
        out_specs=(P("feat", "nodes"), P("feat"), P("feat", None)),
        check_vma=False,
    )
```

time: 447 us -> 295 us (0.66)
  waiting for transfers between devices: 266 us -> 124 us
  matrix products: 43.9 us -> 26.8 us
  blocking collectives: 69 us -> 75.4 us
  local copies, waits for them, and re-layouts: 34.9 us -> 28.6 us
  starting transfers between devices: 13.2 us -> 18 us
    reduce_scatter x1 -> x3, waiting for transfers between devices: 125 us -> 65.5 us  [the longest x1 28.2 us: shards(): lax.psum_scatter(grad_part, 'feat', scatter_dimension=0, tiled=True)]
    all_gather x1, waiting for transfers between devices: 56.1 us -> 0.01 us  [shards(): w1 = lax.all_gather(w_first, 'feat', axis=0, tiled=True)]
    all_gather x0 -> x3, blocking collectives: none -> 37.5 us  [the longest x1 26.5 us: shards(): b1 = lax.all_gather(b_first, 'feat', axis=0, tiled=True)]
    all_to_all x1 -> x0, blocking collectives: 31.3 us -> none  [shards(): lax.all_to_all(own_two[table], 'nodes', split_axis=0, concat_axis=0, tile...]
    psum x1 -> x0, waiting for transfers between devices: 30 us -> none  [shards(): logits = lax.psum(partial_logits, 'feat')]
    dot_general x8, matrix products: 43.4 us -> 23.2 us  [the longest x1 6.91 us: shards(): jnp.einsum('btij,btjf->bif', weights, sources, preferred_element_type=jnp...]
    all_to_all x1 -> x3, waiting for transfers between devices: 6.46 us -> 13.5 us  [the longest x1 7.06 us: shards(): lax.all_to_all(slotsum.reshape(parts, slots, blk, grades), 'nodes', split...]
    gather x6, local copies, waits for them, and re-layouts: 16.2 us -> 9.76 us  [the longest x1 6.56 us: shards(): sources = arrived.reshape(parts * slots, blk, width)[tile_src]]
  transfers between devices with their start and end apart: 6 -> 9, of which waited for: 6 -> 7; matrix products, arithmetic and copies ran while one was open for 1% -> 10% of each run, Pallas kernels for 0% -> 0%
where the time goes in v1:
time: 295 us; the launch traced here: 294 us
  waiting for transfers between devices  124 us (42%)
  blocking collectives  75.4 us (26%)
  local copies, waits for them, and re-layouts  28.6 us (10%)
  matrix products  26.8 us (9%)
  starting transfers between devices  18 us (6%)
  between operations  14.1 us (5%)
  other arithmetic  6.76 us (2%)
    psum x1, blocking collectives, shards(): small = lax.psum(small, 'nodes')  37.9 us
    reduce_scatter x1, waiting for transfers between devices, shards(): lax.psum_scatter(grad_part, 'feat', scatter_dimension=0, tiled=True)  28.2 us
    unnamed x6, waiting for transfers between devices  26.9 us
    all_gather x1, blocking collectives, shards(): b1 = lax.all_gather(b_first, 'feat', axis=0, tiled=True)  26.5 us
    reduce_scatter x1, waiting for transfers between devices, shards(): small = lax.psum_scatter(small, 'feat', scatter_dimension=0, tiled=True)  20.3 us
    all_to_all x1, waiting for transfers between devices, shards(): lax.all_to_all(own_one[table], 'nodes', split_axis=0, concat_axis=0, tile...  18.5 us
    reduce_scatter x1, waiting for transfers between devices, shards(): spread = lax.psum_scatter(spread, 'feat', scatter_dimension=0, tiled=True)  17 us
    all_to_all x1, starting transfers between devices, shards(): lax.all_to_all(own_one[table], 'nodes', split_axis=0, concat_axis=0, tile...  7.28 us
  transfers between devices with their start and end apart: 9, of which 7 were waited for; matrix products, arithmetic and copies ran while one was open for 10% of the time, Pallas kernels for 0%

profile of v1, /device:TPU:0, one launch (start us, length us, event | category | flops | bytes accessed | tf_op | source)
XLA Modules:
  0.0 294.0 jit_solution(2246332280065388524)
XLA Ops:
  8.1 3.2 %gather_fusion.1 = bf16[16,128,256]{2,1,0:T(8,128)(2,1)} fusion(bf16[32,128,256]{2,1,0:T(8,128)(2,1)} %bitcast.87, s32[1024]{0:T(1024)S(1)} %pad_clamp_fusion.2), kind=kCustom, calls=%fused_computation.1 | custom fusion | bytes 2097216 | tf_op jit(solution)/shard_map/gather | solution.py:30
  11.2 7.3 %all-to-all-start = ((bf16[8,2,128,256]{3,2,1,0:T(8,128)(2,1)}), bf16[8,2,128,256]{3,2,1,0:T(8,128)(2,1)S(1)}, u32[]{:S(2)}, u32[]{:S(2)}) async-start(bf16[8,2,128,256]{3,2,1,0:T(8,128)(2,1)} %bitcast.3), calls=%async_computation | async-start | bytes 2097152 | tf_op jit(solution)/shard_map/all_to_all | solution.py:30
  21.2 4.5 %broadcast_multiply_fusion = bf16[32,4,128,128]{3,2,1,0:T(8,128)(2,1)} fusion(bf16[32,4,128,128]{3,2,1,0:T(8,128)(2,1)} %param.13, bf16[32,4]{1,0:T(8,128)(2,1)S(1)} %copy.68), kind=kLoop, calls=%fused_computation.11 | loop fusion | flops 2097152 | bytes 8388864 | tf_op jit(solution)/shard_map/mul | solution.py:22
  25.7 18.5 %all-to-all-done = bf16[8,2,128,256]{3,2,1,0:T(8,128)(2,1)S(1)} async-done(((bf16[8,2,128,256]{3,2,1,0:T(8,128)(2,1)}), bf16[8,2,128,256]{3,2,1,0:T(8,128)(2,1)S(1)}, u32[]{:S(2)}, u32[]{:S(2)}) %all-to-all-start) | async-done | bytes 1048608 | tf_op jit(solution)/shard_map/all_to_all | solution.py:30
  44.3 6.6 %gather_fusion.2 = bf16[128,128,256]{2,1,0:T(8,128)(2,1)} fusion(bf16[16,128,256]{2,1,0:T(8,128)(2,1)S(1)} %bitcast.82, s32[1024]{0:T(1024)S(1)} %pad_clamp_fusion.1), kind=kCustom, calls=%fused_computation.2 | custom fusion | bytes 16777728 | tf_op jit(solution)/shard_map/gather | solution.py:31
  50.8 6.9 %fusion = bf16[32,128,256]{2,1,0:T(8,128)(2,1)S(1)} fusion(bf16[32,128,256]{2,1,0:T(8,128)(2,1)} %bitcast.88, bf16[32,4,128,128]{3,2,1,0:T(8,128)(2,1)} %broadcast_multiply_fusion, bf16[32,4,128,256]{3,2,1,0:T(8,128)(2,1)} %bitcast.83), kind=kOutput, calls=%fused_computation.6 | convolution fusion | flops 1076887552 | bytes 16777216 | tf_op jit(solution)/shard_map/btij,btjf->bif/dot_general | solution.py:32
  57.8 2.5 copy.71
  60.3 3.6 %all-to-all-start.1 = ((bf16[4,1024,256]{1,2,0:T(8,128)(2,1)}), bf16[4,1024,256]{1,2,0:T(8,128)(2,1)S(1)}, u32[]{:S(2)}, u32[]{:S(2)}) async-start(bf16[4,1024,256]{1,2,0:T(8,128)(2,1)} %copy.71), calls=%async_computation.1 | async-start | bytes 4194304 | tf_op jit(solution)/shard_map/all_to_all | solution.py:34
  63.9 26.5 %all-gather = f32[4,1,256]{2,1,0:T(1,128)S(1)} all-gather(f32[1,1,256]{2,1,0:T(1,128)S(1)} %bitcast.100), channel_id=1, replica_groups=mesh['nodes'=8,'feat'=4] {'feat'}, dimensions={0}, use_global_device_ids=true | all-gather | bytes 5120 | tf_op jit(solution)/shard_map/all_gather | solution.py:27
  90.4 5.2 %all_gather.14 = bf16[1024,16]{0,1:T(8,128)(2,1)S(1)} all-gather(bf16[256,16]{0,1:T(8,128)(2,1)S(1)} %copy-done.5), channel_id=1, replica_groups=mesh['nodes'=8,'feat'=4] {'feat'}, dimensions={0}, use_global_device_ids=true | all-gather | bytes 40960 | tf_op jit(solution)/shard_map/all_gather | solution.py:26
  95.6 4.8 %fusion.30 = f32[1024,1024]{1,0:T(8,128)S(1)} fusion(bf16[1024,1024]{0,1:T(8,128)(2,1)S(1)} %bitcast.90, bf16[1024,1024]{1,0:T(8,128)(2,1)} %all-gather.3.cloned.1.call-done), kind=kOutput, calls=%fused_computation.63 | convolution fusion | flops 2147483648 | bytes 8388608 | tf_op jit(solution)/shard_map/dot_general | solution.py:35
  103.0 5.8 %all_gather.15 = f32[4096,16]{0,1:T(8,128)S(1)} all-gather(f32[1024,16]{0,1:T(8,128)S(1)} %fusion.10), channel_id=1, replica_groups=mesh['nodes'=8,'feat'=4] {'feat'}, dimensions={0}, use_global_device_ids=true | all-gather | bytes 327680 | tf_op jit(solution)/shard_map/all_gather | solution.py:39
  110.1 3.6 %all-to-all-start.2 = ((f32[8,2,128,16]{2,3,1,0:T(8,128)}), f32[8,2,128,16]{2,3,1,0:T(8,128)S(1)}, u32[]{:S(2)}, u32[]{:S(2)}) async-start(f32[8,2,128,16]{2,3,1,0:T(8,128)} %bitcast.14), calls=%async_computation.2 | async-start | bytes 262144 | tf_op jit(solution)/shard_map/all_to_all | solution.py:40
  114.8 6.4 %all-to-all-done.2 = f32[8,2,128,16]{2,3,1,0:T(8,128)S(1)} async-done(((f32[8,2,128,16]{2,3,1,0:T(8,128)}), f32[8,2,128,16]{2,3,1,0:T(8,128)S(1)}, u32[]{:S(2)}, u32[]{:S(2)}) %all-to-all-start.2) | async-done | bytes 131104 | tf_op jit(solution)/shard_map/all_to_all | solution.py:40
  129.1 3.4 %all-to-all-start.3 = ((f32[8,2,128,16]{2,3,1,0:T(8,128)}), f32[8,2,128,16]{2,3,1,0:T(8,128)S(1)}, u32[]{:S(2)}, u32[]{:S(2)}) async-start(f32[8,2,128,16]{2,3,1,0:T(8,128)} %copy.81), calls=%async_computation.3 | async-start | bytes 262144 | tf_op jit(solution)/shard_map/all_to_all | solution.py:63
  132.7 7.1 %all-to-all-done.3 = f32[8,2,128,16]{2,3,1,0:T(8,128)S(1)} async-done(((f32[8,2,128,16]{2,3,1,0:T(8,128)}), f32[8,2,128,16]{2,3,1,0:T(8,128)S(1)}, u32[]{:S(2)}, u32[]{:S(2)}) %all-to-all-start.3) | async-done | bytes 131104 | tf_op jit(solution)/shard_map/all_to_all | solution.py:63
  141.7 17.0 %reduce-scatter.7.cloned.1.call-done = f32[8,2048]{1,0:T(8,128)} async-done(((f32[32,2048]{1,0:T(8,128)}), f32[8,2048]{1,0:T(8,128)}) %reduce-scatter.7.cloned.1.call-update) | async-done | bytes 65552 | tf_op jit(solution)/shard_map/reduce_scatter | solution.py:70
  159.9 3.0 %fusion.29 = (f32[1024]{0:T(1024)S(1)}, bf16[1024,1024]{1,0:T(8,128)(2,1)S(1)}) fusion(bf16[1024,16]{0,1:T(8,128)(2,1)S(1)} %add_convert_fusion, bf16[1024,16]{0,1:T(8,128)(2,1)S(1)} %all_gather.14, f32[1024,1024]{1,0:T(8,128)} %copy-done.1, f32[1024]{0:T(1024)S(1)} %bitcast.96), kind=kOutput, calls=%fused_computation.62 | convolution fusion | flops 38796288 | bytes 6365184 | tf_op jit(solution)/shard_map/dot_general | solution.py:75
  163.0 3.7 %fusion.3 = bf16[1024,1024]{1,0:T(8,128)(2,1)} fusion(bf16[1024,1024]{0,1:T(8,128)(2,1)S(1)} %bitcast.91, bf16[1024,1024]{1,0:T(8,128)(2,1)S(1)} %get-tuple-element.8), kind=kOutput, calls=%fused_computation.12 | convolution fusion | flops 2148532224 | bytes 6291456 | tf_op jit(solution)/shard_map/dot_general | solution.py:81
  166.7 2.7 fusion.9
  170.1 28.2 %reduce-scatter.9.cloned.1.call-done = bf16[256,1024]{1,0:T(8,128)(2,1)} async-done(((bf16[1024,1024]{1,0:T(8,128)(2,1)}), bf16[256,1024]{1,0:T(8,128)(2,1)}) %reduce-scatter.9.cloned.1.call-update) | async-done | bytes 524304 | tf_op jit(solution)/shard_map/reduce_scatter | solution.py:84
  200.4 20.3 %reduce-scatter.11.cloned.1.call-done = f32[256,17]{0,1:T(8,128)} async-done(((f32[1024,17]{0,1:T(8,128)}), f32[256,17]{0,1:T(8,128)}) %reduce-scatter.11.cloned.1.call-update) | async-done | bytes 17424 | tf_op jit(solution)/shard_map/reduce_scatter | solution.py:80
  220.7 37.9 %psum.8 = f32[256,17]{0,1:T(8,128)S(1)} all-reduce(f32[256,17]{0,1:T(8,128)} %reduce-scatter.11.cloned.1.call-done), channel_id=1, replica_groups=mesh['nodes'=8,'feat'=4] {'nodes'}, use_global_device_ids=true, to_apply=%region_5.6 | all-reduce | flops 4352 | bytes 34816 | tf_op jit(solution)/shard_map/psum | solution.py:79
  259.7 26.1 %reduce-scatter.13.cloned.1.call-done = bf16[128,256]{1,0:T(8,128)(2,1)} async-done(((bf16[1024,256]{1,0:T(8,128)(2,1)}), bf16[128,256]{1,0:T(8,128)(2,1)}) %reduce-scatter.13.cloned.1.call-update) | async-done | bytes 65552
  (80 shorter events, 25.3 us)
Async XLA Ops:
  7.2 12.5 %copy-start = (s32[1,8]{1,0:T(1,128)S(1)}, s32[1,8]{1,0:T(1,128)}, u32[]{:S(2)}) copy-start(s32[1,8]{1,0:T(1,128)} %param.10) | copy-start | bytes 100
  7.2 12.1 %copy-start.4 = (s32[32,4]{0,1:T(4,128)S(1)}, s32[32,4]{0,1:T(4,128)}, u32[]{:S(2)}) copy-start(s32[32,4]{0,1:T(4,128)} %param.12) | copy-start | bytes 1540
  11.2 33.0 %all-to-all-start = ((bf16[8,2,128,256]{3,2,1,0:T(8,128)(2,1)}), bf16[8,2,128,256]{3,2,1,0:T(8,128)(2,1)S(1)}, u32[]{:S(2)}, u32[]{:S(2)}) async-start(bf16[8,2,128,256]{3,2,1,0:T(8,128)(2,1)} %bitcast.3), calls=%async_computation | async-start | bytes 2097152 | tf_op jit(solution)/shard_map/all_to_all | solution.py:30
  18.5 77.1 %all-gather.3.cloned.1.call-start = ((), (), s32[]{:S(2)}) async-start(), calls=%async_computation.8 | async-start | bytes 2621440 | tf_op jit(solution)/shard_map/all_gather | solution.py:25
  57.8 6.1 %copy-start.7 = (f32[256]{0:T(256)S(1)}, f32[256]{0:T(256)}, u32[]{:S(2)}) copy-start(f32[256]{0:T(256)} %param.16) | copy-start | bytes 3076
  57.8 32.7 %copy-start.5 = (bf16[256,16]{0,1:T(8,128)(2,1)S(1)}, bf16[256,16]{0,1:T(8,128)(2,1)}, u32[]{:S(2)}) copy-start(bf16[256,16]{0,1:T(8,128)(2,1)} %param.17) | copy-start | bytes 24580
  60.3 35.3 %all-to-all-start.1 = ((bf16[4,1024,256]{1,2,0:T(8,128)(2,1)}), bf16[4,1024,256]{1,2,0:T(8,128)(2,1)S(1)}, u32[]{:S(2)}, u32[]{:S(2)}) async-start(bf16[4,1024,256]{1,2,0:T(8,128)(2,1)} %copy.71), calls=%async_computation.1 | async-start | bytes 4194304 | tf_op jit(solution)/shard_map/all_to_all | solution.py:34
  95.6 4.8 %copy-start.2 = (bf16[4,1024,256]{1,2,0:T(8,128)(2,1)}, bf16[4,1024,256]{1,2,0:T(8,128)(2,1)S(1)}, u32[]{:S(2)}) copy-start(bf16[4,1024,256]{1,2,0:T(8,128)(2,1)S(1)} %all-to-all-done.1) | copy-start | bytes 6291460
  100.4 1.9 copy-start.1
  110.1 11.1 %all-to-all-start.2 = ((f32[8,2,128,16]{2,3,1,0:T(8,128)}), f32[8,2,128,16]{2,3,1,0:T(8,128)S(1)}, u32[]{:S(2)}, u32[]{:S(2)}) async-start(f32[8,2,128,16]{2,3,1,0:T(8,128)} %bitcast.14), calls=%async_computation.2 | async-start | bytes 262144 | tf_op jit(solution)/shard_map/all_to_all | solution.py:40
  124.0 8.5 %copy-start.6 = (s32[1,8,2]{1,2,0:T(2,128)S(1)}, s32[1,8,2]{1,2,0:T(2,128)}, u32[]{:S(2)}) copy-start(s32[1,8,2]{1,2,0:T(2,128)} %param.11) | copy-start | bytes 196
  129.1 10.7 %all-to-all-start.3 = ((f32[8,2,128,16]{2,3,1,0:T(8,128)}), f32[8,2,128,16]{2,3,1,0:T(8,128)S(1)}, u32[]{:S(2)}, u32[]{:S(2)}) async-start(f32[8,2,128,16]{2,3,1,0:T(8,128)} %copy.81), calls=%async_computation.3 | async-start | bytes 262144 | tf_op jit(solution)/shard_map/all_to_all | solution.py:63
  132.4 26.2 %reduce-scatter.7.cloned.1.call-start = ((), (), s32[]{:S(2)}) async-start(), calls=%async_computation.9 | async-start | bytes 327680 | tf_op jit(solution)/shard_map/reduce_scatter | solution.py:70
  140.7 22.2 %copy-start.3 = (bf16[4,1024,256]{1,2,0:T(8,128)(2,1)S(1)}, bf16[4,1024,256]{1,2,0:T(8,128)(2,1)}, u32[]{:S(2)}) copy-start(bf16[4,1024,256]{1,2,0:T(8,128)(2,1)} %copy-done.2) | copy-start | bytes 6291460
  141.7 56.6 %reduce-scatter.9.cloned.1.call-start = ((), (), s32[]{:S(2)}) async-start(), calls=%async_computation.10 | async-start | bytes 2621440 | tf_op jit(solution)/shard_map/reduce_scatter | solution.py:84
  166.7 54.0 %reduce-scatter.11.cloned.1.call-start = ((), (), s32[]{:S(2)}) async-start(), calls=%async_computation.11 | async-start | bytes 122880 | tf_op jit(solution)/shard_map/reduce_scatter | solution.py:80
  170.0 115.8 %reduce-scatter.13.cloned.1.call-start = ((), (), s32[]{:S(2)}) async-start(), calls=%async_computation.12 | async-start | bytes 589824
Sparse Core Ops, SparseCore 0:
  20.9 23.9 all-gather.2
  141.8 16.8 reduce-scatter.6
  166.8 31.4 reduce-scatter.8
  201.1 19.5 reduce-scatter.10
  223.9 61.9 reduce-scatter.12

commit v2 on v1

v2 whole, which is shorter than its diff:
```python
import functools
import math

import jax
import jax.numpy as jnp
from jax import lax
from jax.experimental import pallas as pl
from jax.experimental.pallas import tpu as pltpu
from jax.sharding import PartitionSpec as P

MESH = pl.DeviceIdType.MESH
F32 = jnp.float32
BF16 = jnp.bfloat16


def flip(index, mask):
    bit = 1
    while bit <= mask:
        if mask & bit:
            index = index + bit - 2 * bit * ((index // bit) % 2)
        bit *= 2
    return index


def greet(parts, fsize, me_n, me_f):
    barrier = pltpu.get_barrier_semaphore()
    for d in range(1, fsize):
        pl.semaphore_signal(barrier, inc=1, device_id=(me_n, (me_f + d) % fsize), device_id_type=MESH)
    for d in range(1, parts):
        pl.semaphore_signal(barrier, inc=1, device_id=((me_n + d) % parts, me_f), device_id_type=MESH)
    pl.semaphore_wait(barrier, fsize + parts - 2)


def remote(src, dst, send, recv, device):
    return pltpu.make_async_remote_copy(
        src_ref=src, dst_ref=dst, send_sem=send, recv_sem=recv, device_id=device, device_id_type=MESH
    )


def stage_bits(parts, fsize):
    f_bits = [("f", 1 << i) for i in range(fsize.bit_length() - 1)]
    n_bits = [("n", 1 << i) for i in range(parts.bit_length() - 1)]
    first = f_bits + n_bits
    second = f_bits[:1] + n_bits[:1] + f_bits[1:] + n_bits[1:]
    return (first, second)


def kept(bits, done, fsize, parts):
    gone_f = sum(b for a, b in bits[:done] if a == "f")
    gone_n = sum(b for a, b in bits[:done] if a == "n")
    return [(f, n) for f in range(fsize) for n in range(parts) if not (f & gone_f) and not (n & gone_n)]


def later_kernel(
    dims, agg, w1, b1, w2, w2t, tiles, src, live, table, labels, grad_t, small_out,
    mask, mask_t, hidden, pall, sbuf, rbuf, r3, tl, dl, contrib, sback, rback, spread, rspread,
    dproj_t, dpre_t, acc, gout, gin, sm, smin, tile_sem,
    ag_s, ag_r, ex_s, ex_r, bk_s, bk_r, sp_s, sp_r, rs_s, rs_r, sm_s, sm_r,
):
    parts, fsize, slots, nblocks, per_block, blk, grades, scale = dims
    me_n, me_f = lax.axis_index("nodes"), lax.axis_index("feat")
    mine = nblocks // fsize
    rows, hid = hidden.shape
    width = rows // 4
    fw = agg.shape[1] // fsize
    hb = hid // parts
    half = fw // 2
    base = me_f * mine

    fetch = pltpu.make_async_copy(tiles.at[pl.ds(base, mine)], tl, tile_sem)
    fetch.start()
    greet(parts, fsize, me_n, me_f)

    @pl.loop(0, 4)
    def _(r):
        at = pl.ds(pl.multiple_of(r * width, width), width)
        pre = jnp.dot(agg[at, :], w1[...], preferred_element_type=F32) + b1[...]
        hb16 = jnp.maximum(pre, 0.0).astype(BF16)
        hidden[at, :] = hb16
        mask[at, :] = jnp.where(pre > 0, 1.0, 0.0).astype(BF16)
        pt = lax.dot_general(w2t[...], hb16, (((1,), (1,)), ((), ())), preferred_element_type=F32)
        for i in range(width // blk):
            pall[base + r * (width // blk) + i] = pt[:, i * blk : (i + 1) * blk]

    copies = []
    for d in range(1, fsize):
        own = pall.at[pl.ds(base, mine)]
        c = remote(own, own, ag_s.at[d], ag_r.at[d], (me_n, (me_f + d) % fsize))
        c.start()
        copies.append(c)
    fetch.wait()

    @pl.loop(0, 4)
    def _(r):
        at = pl.ds(pl.multiple_of(r * width, width), width)
        mask_t[:, at] = mask[at, :].T

    for c in copies:
        c.wait()
    for p in range(parts):
        for s in range(slots):
            sbuf[p, s] = pall[table[p, s]]
    rbuf[me_n] = sbuf[me_n]
    copies = []
    for d in range(1, parts):
        p = (me_n + d) % parts
        c = remote(sbuf.at[p], rbuf.at[me_n], ex_s.at[d], ex_r.at[d], (p, me_f))
        c.start()
        copies.append(c)
    for c in copies:
        c.wait()
    for p in range(parts):
        for s in range(slots):
            x = rbuf[p, s]
            hi = x.astype(BF16)
            rest = x - hi.astype(F32)
            mid = rest.astype(BF16)
            low = (rest - mid.astype(F32)).astype(BF16)
            r3[p * slots + s] = jnp.concatenate([hi, mid, low], axis=0)

    grade_id = lax.broadcasted_iota(jnp.int32, (grades, blk), 0)

    @pl.loop(0, mine)
    def _(b):
        pieces = [r3[src[base + b, k]] * live[base + b, k].astype(BF16) for k in range(per_block)]
        lhs = jnp.concatenate(pieces, axis=1)
        wcat = jnp.concatenate([tl[b, k] for k in range(per_block)], axis=1)
        out = lax.dot_general(lhs, wcat, (((1,), (1,)), ((), ())), preferred_element_type=F32)
        logits = pall[base + b] + (
            out[:grades] + (out[grades : 2 * grades] + out[2 * grades : 3 * grades])
        )
        expo = jnp.exp(logits)
        probs = expo / jnp.sum(expo, axis=0, keepdims=True)
        onehot = jnp.where(labels[pl.ds(base + b, 1), :] == grade_id, 1.0, 0.0)
        dlog = (probs - onehot) * scale
        dl[b] = dlog
        back = jnp.dot(dlog.astype(BF16), wcat, preferred_element_type=F32)
        for k in range(per_block):
            contrib[b * per_block + k] = back[:, k * blk : (k + 1) * blk] * live[base + b, k]

    @pl.loop(0, parts)
    def _(p):
        for s in range(slots):
            slot = p * slots + s
            total = jnp.zeros((grades, blk), F32)
            for b in range(mine):
                for k in range(per_block):
                    hit = jnp.where(src[base + b, k] == slot, 1.0, 0.0)
                    total = total + contrib[b * per_block + k] * hit
            sback[p, s] = total

    rback[me_n] = sback[me_n]
    copies = []
    for d in range(1, parts):
        p = (me_n + d) % parts
        c = remote(sback.at[p], rback.at[me_n], bk_s.at[d], bk_r.at[d], (p, me_f))
        c.start()
        copies.append(c)
    for c in copies:
        c.wait()

    @pl.loop(0, nblocks)
    def _(b):
        total = jnp.zeros((grades, blk), F32)
        for p in range(parts):
            for s in range(slots):
                hit = jnp.where(table[p, s] == b, 1.0, 0.0)
                total = total + rback[p, s] * hit
        spread[b] = total

    copies = []
    for d in range(1, fsize):
        to = (me_f + d) % fsize
        c = remote(
            spread.at[pl.ds(to * mine, mine)], rspread.at[d - 1], sp_s.at[d], sp_r.at[d], (me_n, to)
        )
        c.start()
        copies.append(c)
    for c in copies:
        c.wait()
    for b in range(mine):
        total = spread[base + b]
        for d in range(fsize - 1):
            total = total + rspread[d, b]
        dproj_t[:, b * blk : (b + 1) * blk] = (dl[b] + total).astype(BF16)

    for n in range(parts):
        at = pl.ds(pl.multiple_of(flip(me_n, n) * hb, hb), hb)
        d = jnp.dot(w2[at, :], dproj_t[...], preferred_element_type=F32)
        dpre_t[n * hb : (n + 1) * hb, :] = jnp.where(mask_t[at, :] > 0, d, 0.0).astype(BF16)

    orders = stage_bits(parts, fsize)
    stages = len(orders[0])
    sizes = [(fsize * parts) >> (t + 1) for t in range(stages)]
    starts = [sum(sizes[:t]) for t in range(stages)]

    def product(f):
        at = pl.ds(pl.multiple_of(flip(me_f, f) * fw, fw), fw)
        return jnp.dot(dpre_t[...], agg[:, at], preferred_element_type=F32)

    def partner(axis, bit):
        return (flip(me_n, bit), me_f) if axis == "n" else (me_n, flip(me_f, bit))

    def launch(c, t):
        at = pl.ds(starts[t], sizes[t])
        r = remote(gout.at[c, at], gin.at[c, at], rs_s.at[c, t], rs_r.at[c, t], partner(*orders[c][t]))
        r.start()
        return r

    def going(c, t):
        axis, bit = orders[c][t]
        return [j for j in kept(orders[c], t, fsize, parts) if (j[0] if axis == "f" else j[1]) & bit]

    flying = [None, None]
    for f in range(fsize):
        if f & 1:
            g = product(f).astype(BF16)
            for c in range(2):
                for i, j in enumerate(going(c, 0)):
                    if j[0] == f:
                        gout[c, i] = g[j[1] * hb : (j[1] + 1) * hb, c * half : (c + 1) * half]
    for c in range(2):
        flying[c] = launch(c, 0)
    for f in range(fsize):
        if not f & 1:
            g = product(f)
            for c in range(2):
                for n in range(parts):
                    acc[c, f, n] = g[n * hb : (n + 1) * hb, c * half : (c + 1) * half]

    both = jnp.dot(dproj_t[...], hidden[...], preferred_element_type=F32)
    bias = jnp.sum(
        w2t[...].astype(F32) * jnp.dot(dproj_t[...], mask[...], preferred_element_type=F32),
        axis=0,
        keepdims=True,
    )
    small_full = jnp.concatenate([both, jnp.broadcast_to(bias, (8, hid))], axis=0)
    rel = [small_full[:, g * fw : (g + 1) * fw] for g in range(fsize)]
    for f in range(fsize):
        pick = flip(me_f, f)
        total = rel[0]
        for g in range(1, fsize):
            total = jnp.where(pick == g, rel[g], total)
        sm[f] = total

    small_bits = orders[0]
    at_small = 0
    for t in range(stages):
        axis, bit = small_bits[t]
        if axis == "f":
            idx = [f for f in range(fsize) if not f & (bit - 1) and f & bit]
        else:
            idx = [0]
        smalls = []
        for f in idx:
            r = remote(sm.at[f], smin.at[at_small], sm_s.at[at_small], sm_r.at[at_small], partner(axis, bit))
            r.start()
            smalls.append((f - bit if axis == "f" else 0, at_small, r))
            at_small += 1
        for c in range(2):
            flying[c].wait()
            sent = going(c, t)
            axis_c, bit_c = orders[c][t]
            for i, j in enumerate(sent):
                k = (j[0] - bit_c, j[1]) if axis_c == "f" else (j[0], j[1] - bit_c)
                new = acc[c, k[0], k[1]] + gin[c, starts[t] + i].astype(F32)
                nxt = going(c, t + 1) if t + 1 < stages else []
                if k in nxt:
                    gout[c, starts[t + 1] + nxt.index(k)] = new.astype(BF16)
                elif t + 1 < stages:
                    acc[c, k[0], k[1]] = new
                else:
                    grad_t[:, c * half : (c + 1) * half] = new
            if t + 1 < stages:
                flying[c] = launch(c, t + 1)
        for _, _, r in smalls:
            r.wait()
        for f, slot, _ in smalls:
            sm[f] = sm[f] + smin[slot]
    small_out[...] = sm[0]


def later(dims, agg, w1, b1, w2, tiles, src, live, table, labels):
    parts, fsize, slots, nblocks, per_block, blk, grades, scale = dims
    mine = nblocks // fsize
    rows, feats = agg.shape
    hid = w1.shape[1]
    fw, hb = feats // fsize, hid // parts
    stages = len(stage_bits(parts, fsize)[0])
    tiles_sent = fsize * parts - 1
    n_small = (fsize - 1) + (parts.bit_length() - 1)
    vm = pl.BlockSpec(memory_space=pltpu.VMEM)
    sc = pl.BlockSpec(memory_space=pltpu.SMEM)
    dma = pltpu.SemaphoreType.DMA
    field = (grades, blk)
    return pl.pallas_call(
        functools.partial(later_kernel, dims),
        out_shape=(
            jax.ShapeDtypeStruct((hb, fw), F32),
            jax.ShapeDtypeStruct((grades + 8, fw), F32),
        ),
        in_specs=[vm, vm, vm, vm, vm, pl.BlockSpec(memory_space=pl.ANY), sc, sc, sc, vm],
        out_specs=(vm, vm),
        scratch_shapes=[
            pltpu.VMEM((rows, hid), BF16),
            pltpu.VMEM((hid, rows), BF16),
            pltpu.VMEM((rows, hid), BF16),
            pltpu.VMEM((nblocks,) + field, F32),
            pltpu.VMEM((parts, slots) + field, F32),
            pltpu.VMEM((parts, slots) + field, F32),
            pltpu.VMEM((parts * slots, 3 * grades, blk), BF16),
            pltpu.VMEM((mine, per_block, blk, blk), BF16),
            pltpu.VMEM((mine,) + field, F32),
            pltpu.VMEM((mine * per_block,) + field, F32),
            pltpu.VMEM((parts, slots) + field, F32),
            pltpu.VMEM((parts, slots) + field, F32),
            pltpu.VMEM((nblocks,) + field, F32),
            pltpu.VMEM((fsize - 1, mine) + field, F32),
            pltpu.VMEM((grades, rows), BF16),
            pltpu.VMEM((hid, rows), BF16),
            pltpu.VMEM((2, fsize, parts, hb, fw // 2), F32),
            pltpu.VMEM((2, tiles_sent, hb, fw // 2), BF16),
            pltpu.VMEM((2, tiles_sent, hb, fw // 2), BF16),
            pltpu.VMEM((fsize, grades + 8, fw), F32),
            pltpu.VMEM((n_small, grades + 8, fw), F32),
            dma,
            dma((fsize,)), dma((fsize,)),
            dma((parts,)), dma((parts,)),
            dma((parts,)), dma((parts,)),
            dma((fsize,)), dma((fsize,)),
            dma((2, stages)), dma((2, stages)),
            dma((n_small,)), dma((n_small,)),
        ],
        compiler_params=pltpu.CompilerParams(
            collective_id=1, has_side_effects=True, vmem_limit_bytes=56 * 1024 * 1024
        ),
        cost_estimate=pl.CostEstimate(
            flops=4 * rows * hid * feats, bytes_accessed=6 * rows * hid, transcendentals=rows * grades
        ),
    )(agg, w1, b1, w2, w2.T, tiles, src, live, table, labels)


def shards(features, pair_count, send_blocks, tile_src, tiles, labels, w_first, b_first, w_second):
    rows, width = features.shape
    nblocks, per_block = tile_src.shape
    blk = tiles.shape[2]
    parts = lax.axis_size("nodes")
    fsize = lax.axis_size("feat")
    slots = send_blocks.shape[2]
    grades = w_second.shape[1]
    live = (tile_src % slots) < pair_count[0][tile_src // slots]
    weights = tiles * live[:, :, None, None].astype(BF16)
    table = send_blocks[0]

    w1 = lax.all_gather(w_first, "feat", axis=0, tiled=True)
    w2 = lax.all_gather(w_second, "feat", axis=0, tiled=True)
    b1 = lax.all_gather(b_first, "feat", axis=0, tiled=True)

    own_one = features.reshape(nblocks, blk, width)
    arrived = lax.all_to_all(own_one[table], "nodes", split_axis=0, concat_axis=0, tiled=True)
    sources = arrived.reshape(parts * slots, blk, width)[tile_src]
    summed = jnp.einsum("btij,btjf->bif", weights, sources, preferred_element_type=F32)
    agg = (summed + own_one).astype(BF16).reshape(rows, width)
    agg = lax.all_to_all(agg, "feat", split_axis=0, concat_axis=1, tiled=True)

    dims = (parts, fsize, slots, nblocks, per_block, blk, grades, 1.0 / math.sqrt(rows * parts))
    grad_t, small = later(
        dims, agg, w1, b1[None, :], w2, tiles, tile_src, live.astype(F32), table,
        labels.reshape(nblocks, blk),
    )
    return (grad_t.T, small[grades], small[:grades].T)


def solution(mesh):
    placed = (
        P("nodes", "feat"),
        P("nodes", None),
        P("nodes", None, None),
        P("nodes", None),
        P("nodes", None, None, None),
        P("nodes"),
        P("feat", None),
        P("feat"),
        P("feat", None),
    )
    return jax.shard_map(
        shards,
        mesh=mesh,
        in_specs=placed,
        out_specs=(P("feat", "nodes"), P("feat"), P("feat", None)),
        check_vma=False,
    )
```

time: 295 us -> 166 us (0.56)
  waiting for transfers between devices: 124 us -> 23.3 us
  Pallas kernels: 0 us -> 56.2 us
  blocking collectives: 75.4 us -> 32.2 us
  matrix products: 26.8 us -> 7.82 us
  local copies, waits for them, and re-layouts: 28.6 us -> 19.1 us
  starting transfers between devices: 18 us -> 11.1 us
  other arithmetic: 6.76 us -> 1.36 us
    reduce_scatter x3 -> x0, waiting for transfers between devices: 65.5 us -> none  [the longest x1 28.2 us: shards(): lax.psum_scatter(grad_part, 'feat', scatter_dimension=0, tiled=True)]
    pallas_call x0 -> x1, Pallas kernels: none -> 56.2 us  [later(): pl.pallas_call(functools.partial(later_kernel, dims), out_shape=(jax.Shap...]
    psum x1 -> x0, blocking collectives: 37.9 us -> none  [shards(): small = lax.psum(small, 'nodes')]
    unnamed x6 -> x1, waiting for transfers between devices: 26.9 us -> 0.68 us
    all_gather x1, blocking collectives: 5.18 us -> 26.7 us  [shards(): w2 = lax.all_gather(w_second, 'feat', axis=0, tiled=True)]
    all_gather x1, blocking collectives: 26.5 us -> 5.5 us  [shards(): b1 = lax.all_gather(b_first, 'feat', axis=0, tiled=True)]
    dot_general x10 -> x1, matrix products: 26.8 us -> 7.82 us  [shards(): jnp.einsum('btij,btjf->bif', weights, sources, preferred_element_type=F32)]
    all_to_all x2 -> x0, waiting for transfers between devices: 13.5 us -> none  [the longest x1 7.06 us: shards(): lax.all_to_all(slotsum.reshape(parts, slots, blk, grades), 'nodes', split...]
  transfers between devices with their start and end apart: 9 -> 3, of which waited for: 7 -> 1; matrix products, arithmetic and copies ran while one was open for 10% -> 12% of each run, Pallas kernels for 0% -> 0%
where the time goes in v2:
time: 166 us; the launch traced here: 165 us
  Pallas kernels  56.2 us (34%)
  blocking collectives  32.2 us (19%)
  waiting for transfers between devices  23.3 us (14%)
  local copies, waits for them, and re-layouts  19.1 us (12%)
  between operations  14.1 us (8%)
  starting transfers between devices  11.1 us (7%)
  matrix products  7.82 us (5%)
    pallas_call x1, Pallas kernels, later(): pl.pallas_call(functools.partial(later_kernel, dims), out_shape=(jax.Shap...  56.2 us
    all_gather x1, blocking collectives, shards(): w2 = lax.all_gather(w_second, 'feat', axis=0, tiled=True)  26.7 us
    all_to_all x1, waiting for transfers between devices, shards(): lax.all_to_all(own_one[table], 'nodes', split_axis=0, concat_axis=0, tile...  22.6 us
    dot_general x1, matrix products, shards(): jnp.einsum('btij,btjf->bif', weights, sources, preferred_element_type=F32)  7.82 us
    all_to_all x1, starting transfers between devices, shards(): lax.all_to_all(own_one[table], 'nodes', split_axis=0, concat_axis=0, tile...  7.28 us
    gather x1, local copies, waits for them, and re-layouts, shards(): sources = arrived.reshape(parts * slots, blk, width)[tile_src]  6.57 us
    all_gather x1, blocking collectives, shards(): b1 = lax.all_gather(b_first, 'feat', axis=0, tiled=True)  5.5 us
    all_to_all x1, starting transfers between devices, shards(): agg = lax.all_to_all(agg, 'feat', split_axis=0, concat_axis=1, tiled=True)  3.74 us
  transfers between devices with their start and end apart: 3, of which 1 were waited for; matrix products, arithmetic and copies ran while one was open for 12% of the time, Pallas kernels for 0%

profile of v2, /device:TPU:0, one launch (start us, length us, event | category | flops | bytes accessed | tf_op | source)
XLA Modules:
  0.0 165.1 jit_solution(7008180985532083406)
XLA Ops:
  7.2 0.7 compare_select_fusion.2
  8.1 3.2 %gather_fusion.1 = bf16[16,128,256]{2,1,0:T(8,128)(2,1)} fusion(bf16[32,128,256]{2,1,0:T(8,128)(2,1)} %bitcast.34, s32[1024]{0:T(1024)S(1)} %pad_clamp_fusion.1), kind=kCustom, calls=%fused_computation.1 | custom fusion | bytes 2097216 | tf_op jit(solution)/shard_map/gather | solution.py:360
  11.3 7.3 %all-to-all-start = ((bf16[8,2,128,256]{3,2,1,0:T(8,128)(2,1)}), bf16[8,2,128,256]{3,2,1,0:T(8,128)(2,1)S(1)}, u32[]{:S(2)}, u32[]{:S(2)}) async-start(bf16[8,2,128,256]{3,2,1,0:T(8,128)(2,1)} %bitcast.3), calls=%async_computation | async-start | bytes 2097152 | tf_op jit(solution)/shard_map/all_to_all | solution.py:360
  18.6 0.7 all-gather.3.cloned.1.call-update
  19.3 0.1 copy.51.src
  19.4 0.1 copy.56
  19.5 0.1 reshape.55
  19.6 1.2 gather_fusion
  20.8 0.1 reshape.54
  21.0 0.6 fusion.9
  21.6 0.1 reshape.71
  21.7 22.6 %all-to-all-done = bf16[8,2,128,256]{3,2,1,0:T(8,128)(2,1)S(1)} async-done(((bf16[8,2,128,256]{3,2,1,0:T(8,128)(2,1)}), bf16[8,2,128,256]{3,2,1,0:T(8,128)(2,1)S(1)}, u32[]{:S(2)}, u32[]{:S(2)}) %all-to-all-start) | async-done | bytes 1048608 | tf_op jit(solution)/shard_map/all_to_all | solution.py:360
  44.3 6.6 %gather_fusion.2 = bf16[128,128,256]{2,1,0:T(8,128)(2,1)} fusion(bf16[16,128,256]{2,1,0:T(8,128)(2,1)S(1)} %bitcast.29, s32[1024]{0:T(1024)S(1)} %pad_clamp_fusion), kind=kCustom, calls=%fused_computation.2 | custom fusion | bytes 16777728 | tf_op jit(solution)/shard_map/gather | solution.py:361
  50.9 7.8 %fusion = bf16[32,128,256]{2,1,0:T(8,128)(2,1)} fusion(bf16[32,128,256]{2,1,0:T(8,128)(2,1)S(1)} %bitcast.35, bf16[32,4,128,256]{3,2,1,0:T(8,128)(2,1)} %bitcast.30, bf16[32,4,128,128]{3,2,1,0:T(8,128)(2,1)} %tiles.1, bf16[32,4]{1,0:T(8,128)(2,1)S(1)} %convert_element_type.13), kind=kOutput, calls=%fused_computation.4 | convolution fusion | flops 1078984704 | bytes 16777472 | tf_op jit(solution)/shard_map/btij,btjf->bif/dot_general | solution.py:362
  58.7 3.7 %all-to-all-start.1 = ((bf16[4,1024,256]{2,1,0:T(8,128)(2,1)}), bf16[4,1024,256]{2,1,0:T(8,128)(2,1)S(1)}, u32[]{:S(2)}, u32[]{:S(2)}) async-start(bf16[4,1024,256]{2,1,0:T(8,128)(2,1)} %bitcast.33), calls=%async_computation.1 | async-start | bytes 4194304 | tf_op jit(solution)/shard_map/all_to_all | solution.py:364
  62.5 26.7 %all_gather.11 = bf16[1024,16]{0,1:T(8,128)(2,1)S(1)} all-gather(bf16[256,16]{0,1:T(8,128)(2,1)S(1)} %copy-done.4), channel_id=1, replica_groups=mesh['nodes'=8,'feat'=4] {'feat'}, dimensions={0}, use_global_device_ids=true | all-gather | bytes 40960 | tf_op jit(solution)/shard_map/all_gather | solution.py:356
  89.2 0.8 copy.59.w2
  90.0 0.7 copy.61.table
  90.7 5.5 %all-gather = f32[4,1,256]{2,1,0:T(1,128)} all-gather(f32[1,1,256]{2,1,0:T(1,128)S(1)} %bitcast.40), channel_id=1, replica_groups=mesh['nodes'=8,'feat'=4] {'feat'}, dimensions={0}, use_global_device_ids=true | all-gather | bytes 5120 | tf_op jit(solution)/shard_map/all_gather | solution.py:357
  96.2 1.6 copy.64
  97.8 56.2 %shard_map.112 = (f32[128,256]{1,0:T(8,128)}, f32[24,256]{1,0:T(8,128)}) custom-call(bf16[1024,1024]{1,0:T(8,128)(2,1)} %bitcast.32, bf16[1024,1024]{1,0:T(8,128)(2,1)} %all-gather.3.cloned.1.call-done.w1, f32[1,1024]{1,0:T(1,128)} %bitcast.38, bf16[1024,16]{1,0:T(8,128)(2,1)} %copy.59.w2, bf16[16,1024]{1,0:T(8,128)(2,1)} %bitcast.36, ...), custom_call_target="tpu_custom_call" | custom-call | flops 4294967296 | bytes 6291456 | tf_op jit(solution)/shard_map/pallas_call | solution.py:296
  154.1 1.3 slice_bitcast_fusion
  155.4 1.3 slice.6
  156.6 1.7 %copy.62 = f32[256,128]{1,0:T(8,128)} copy(f32[256,128]{0,1:T(8,128)} %bitcast.37) | data formatting | bytes 262144
  (27 shorter events, 0.3 us)
Async XLA Ops:
  7.2 12.4 %copy-start = (s32[1,8]{1,0:T(1,128)S(1)}, s32[1,8]{1,0:T(1,128)}, u32[]{:S(2)}) copy-start(s32[1,8]{1,0:T(1,128)} %param.10) | copy-start | bytes 100
  7.2 12.1 %copy-start.5 = (s32[32,4]{0,1:T(4,128)S(1)}, s32[32,4]{0,1:T(4,128)}, u32[]{:S(2)}) copy-start(s32[32,4]{0,1:T(4,128)} %param.12) | copy-start | bytes 1540
  11.3 33.0 %all-to-all-start = ((bf16[8,2,128,256]{3,2,1,0:T(8,128)(2,1)}), bf16[8,2,128,256]{3,2,1,0:T(8,128)(2,1)S(1)}, u32[]{:S(2)}, u32[]{:S(2)}) async-start(bf16[8,2,128,256]{3,2,1,0:T(8,128)(2,1)} %bitcast.3), calls=%async_computation | async-start | bytes 2097152 | tf_op jit(solution)/shard_map/all_to_all | solution.py:360
  18.5 79.3 %all-gather.3.cloned.1.call-start = ((), (), s32[]{:S(2)}) async-start(), calls=%async_computation.2 | async-start | bytes 2621440 | tf_op jit(solution)/shard_map/all_gather | solution.py:355
  19.4 1.6 copy-start.2
  44.3 6.6 %copy-start.1 = (bf16[4096,256]{1,0:T(8,128)(2,1)S(1)}, bf16[4096,256]{1,0:T(8,128)(2,1)}, u32[]{:S(2)}) copy-start(bf16[4096,256]{1,0:T(8,128)(2,1)} %param.9) | copy-start | bytes 6291460
  58.7 3.8 %copy-start.4 = (bf16[256,16]{0,1:T(8,128)(2,1)S(1)}, bf16[256,16]{0,1:T(8,128)(2,1)}, u32[]{:S(2)}) copy-start(bf16[256,16]{0,1:T(8,128)(2,1)} %param.17) | copy-start | bytes 24580
  58.7 31.3 %copy-start.6 = (s32[1,8,2]{1,2,0:T(2,128)S(1)}, s32[1,8,2]{1,2,0:T(2,128)}, u32[]{:S(2)}) copy-start(s32[1,8,2]{1,2,0:T(2,128)} %param.11) | copy-start | bytes 196
  58.7 32.0 %copy-start.7 = (f32[256]{0:T(256)S(1)}, f32[256]{0:T(256)}, u32[]{:S(2)}) copy-start(f32[256]{0:T(256)} %param.16) | copy-start | bytes 3076
  58.7 37.5 %all-to-all-start.1 = ((bf16[4,1024,256]{2,1,0:T(8,128)(2,1)}), bf16[4,1024,256]{2,1,0:T(8,128)(2,1)S(1)}, u32[]{:S(2)}, u32[]{:S(2)}) async-start(bf16[4,1024,256]{2,1,0:T(8,128)(2,1)} %bitcast.33), calls=%async_computation.1 | async-start | bytes 4194304 | tf_op jit(solution)/shard_map/all_to_all | solution.py:364
  89.2 8.7 %copy-start.3 = (bf16[1024,16]{0,1:T(8,128)(2,1)}, bf16[1024,16]{0,1:T(8,128)(2,1)S(1)}, u32[]{:S(2)}) copy-start(bf16[1024,16]{0,1:T(8,128)(2,1)S(1)} %all_gather.11) | copy-start | bytes 98308
Sparse Core Ops, SparseCore 0:
  20.9 23.9 all-gather.2

commit v3 on v2

--- a/solution.py
+++ b/solution.py
@@ -51,10 +51,12 @@
     return [(f, n) for f in range(fsize) for n in range(parts) if not (f & gone_f) and not (n & gone_n)]
 
 
-def later_kernel(
-    dims, agg, w1, b1, w2, w2t, tiles, src, live, table, labels, grad_t, small_out,
+def whole_kernel(
+    dims, feats_in, w_in, b_in, w2_in, tiles, src, count, table, labels, grad_out, bias_out, second_out,
+    agg, w1, w2, b_all, w2t, b1, fsend, frecv_a, frecv_b, abuf,
     mask, mask_t, hidden, pall, sbuf, rbuf, r3, tl, dl, contrib, sback, rback, spread, rspread,
     dproj_t, dpre_t, acc, gout, gin, sm, smin, tile_sem,
+    w_s, w_r, w2_s, w2_r, b_s, b_r, fx_s, fx_r, tr_s, tr_r,
     ag_s, ag_r, ex_s, ex_r, bk_s, bk_r, sp_s, sp_r, rs_s, rs_r, sm_s, sm_r,
 ):
     parts, fsize, slots, nblocks, per_block, blk, grades, scale = dims
@@ -67,9 +69,123 @@
     half = fw // 2
     base = me_f * mine
 
-    fetch = pltpu.make_async_copy(tiles.at[pl.ds(base, mine)], tl, tile_sem)
+    def live(b, k):
+        slot = src[b, k]
+        return jnp.where(slot % slots < count[0, slot // slots], 1.0, 0.0)
+
+    fetch = pltpu.make_async_copy(tiles, tl, tile_sem)
     fetch.start()
+    frecv = (frecv_a, frecv_b)
+    own_w = pl.ds(pl.multiple_of(me_f * fw, fw), fw)
+    w1[own_w, :] = w_in[...]
+    w2[own_w, :] = jnp.zeros((fw, blk), BF16)
+    w2[own_w, :grades] = w2_in[...]
+    b_all[me_f] = jnp.broadcast_to(b_in[...], (8, fw))
     greet(parts, fsize, me_n, me_f)
+
+    def column(c):
+        return slice(c * half, (c + 1) * half)
+
+    def exchange(c, d):
+        p = (me_n + d) % parts
+        return remote(fsend.at[c, p], frecv[c].at[me_n], fx_s.at[c, d], fx_r.at[c, d], (p, me_f))
+
+    def stage_block(c, p, s):
+        fsend[c, p, s] = feats_in[table[0, p, s], :, column(c)]
+
+    for p in range(parts):
+        for s in range(slots):
+            stage_block(0, p, s)
+    first = []
+    for d in range(1, parts):
+        x = exchange(0, d)
+        x.start()
+        first.append(x)
+
+    def pass_on(j, bit, slot):
+        at = pl.ds(pl.multiple_of(flip(me_f, j) * fw, fw), fw)
+        return remote(w1.at[at, :], w1.at[at, :], w_s.at[slot], w_r.at[slot], (me_n, flip(me_f, bit)))
+
+    weights_flying = []
+    far = []
+    for j in range(1, fsize):
+        if j & (j - 1) == 0:
+            x = pass_on(0, j, j)
+            x.start()
+            (far if j > 1 else weights_flying).append(x)
+    for d in range(1, fsize):
+        to = (me_n, (me_f + d) % fsize)
+        x = remote(w2.at[own_w, :], w2.at[own_w, :], w2_s.at[d], w2_r.at[d], to)
+        x.start()
+        y = remote(b_all.at[me_f], b_all.at[me_f], b_s.at[d], b_r.at[d], to)
+        y.start()
+        weights_flying += [x, y]
+
+    for p in range(parts):
+        for s in range(slots):
+            stage_block(1, p, s)
+    frecv_a[me_n] = fsend[0, me_n]
+    frecv_b[me_n] = fsend[1, me_n]
+    second = []
+    for d in range(1, parts):
+        first[d - 1].wait_send()
+        x = exchange(1, d)
+        x.start()
+        second.append(x)
+    fetch.wait()
+    for x in first:
+        x.wait_recv()
+
+    order = list(range(fsize - 1, -1, -1))
+
+    def aggregate(c):
+        def block(b):
+            wcat = jnp.concatenate([tl[b, k] * live(b, k).astype(BF16) for k in range(per_block)], axis=1)
+            got = jnp.concatenate(
+                [frecv[c][src[b, k] // slots, src[b, k] % slots] for k in range(per_block)], axis=0
+            )
+            total = jnp.dot(wcat, got, preferred_element_type=F32)
+            return (total + feats_in[b, :, column(c)].astype(F32)).astype(BF16)
+
+        lanes = pl.ds(pl.multiple_of(me_f * fw + c * half, half), half)
+        sent = []
+        for j in order:
+            group = flip(me_f, j)
+
+            @pl.loop(0, mine)
+            def _(i):
+                got = block(group * mine + i)
+                if j:
+                    abuf[c, pl.ds(pl.multiple_of((group * mine + i) * blk, blk), blk), :] = got
+                else:
+                    agg[pl.ds(pl.multiple_of(i * blk, blk), blk), lanes] = got
+
+            if j:
+                at = pl.ds(pl.multiple_of(group * rows, rows), rows)
+                x = remote(abuf.at[c, at, :], agg.at[:, lanes], tr_s.at[c, j], tr_r.at[c, j], (me_n, group))
+                x.start()
+                sent.append(x)
+        return sent
+
+    turned = aggregate(0)
+    for x in far:
+        x.wait()
+    for j in range(3, fsize):
+        low = j & -j
+        if j != low:
+            x = pass_on(j - low, low, j)
+            x.start()
+            weights_flying.append(x)
+    for x in second:
+        x.wait()
+    turned += aggregate(1)
+    for x in weights_flying:
+        x.wait()
+    for f in range(fsize):
+        b1[:, f * fw : (f + 1) * fw] = b_all[f, :1, :]
+    w2t[...] = w2[...].T[:grades]
+    for x in turned:
+        x.wait()
 
     @pl.loop(0, 4)
     def _(r):
@@ -88,7 +204,6 @@
         c = remote(own, own, ag_s.at[d], ag_r.at[d], (me_n, (me_f + d) % fsize))
         c.start()
         copies.append(c)
-    fetch.wait()
 
     @pl.loop(0, 4)
     def _(r):
@@ -99,7 +214,7 @@
         c.wait()
     for p in range(parts):
         for s in range(slots):
-            sbuf[p, s] = pall[table[p, s]]
+            sbuf[p, s] = pall[table[0, p, s]]
     rbuf[me_n] = sbuf[me_n]
     copies = []
     for d in range(1, parts):
@@ -122,9 +237,9 @@
 
     @pl.loop(0, mine)
     def _(b):
-        pieces = [r3[src[base + b, k]] * live[base + b, k].astype(BF16) for k in range(per_block)]
+        pieces = [r3[src[base + b, k]] * live(base + b, k).astype(BF16) for k in range(per_block)]
         lhs = jnp.concatenate(pieces, axis=1)
-        wcat = jnp.concatenate([tl[b, k] for k in range(per_block)], axis=1)
+        wcat = jnp.concatenate([tl[base + b, k] for k in range(per_block)], axis=1)
         out = lax.dot_general(lhs, wcat, (((1,), (1,)), ((), ())), preferred_element_type=F32)
         logits = pall[base + b] + (
             out[:grades] + (out[grades : 2 * grades] + out[2 * grades : 3 * grades])
@@ -136,7 +251,7 @@
         dl[b] = dlog
         back = jnp.dot(dlog.astype(BF16), wcat, preferred_element_type=F32)
         for k in range(per_block):
-            contrib[b * per_block + k] = back[:, k * blk : (k + 1) * blk] * live[base + b, k]
+            contrib[b * per_block + k] = back[:, k * blk : (k + 1) * blk] * live(base + b, k)
 
     @pl.loop(0, parts)
     def _(p):
@@ -164,7 +279,7 @@
         total = jnp.zeros((grades, blk), F32)
         for p in range(parts):
             for s in range(slots):
-                hit = jnp.where(table[p, s] == b, 1.0, 0.0)
+                hit = jnp.where(table[0, p, s] == b, 1.0, 0.0)
                 total = total + rback[p, s] * hit
         spread[b] = total
 
@@ -186,7 +301,7 @@
 
     for n in range(parts):
         at = pl.ds(pl.multiple_of(flip(me_n, n) * hb, hb), hb)
-        d = jnp.dot(w2[at, :], dproj_t[...], preferred_element_type=F32)
+        d = jnp.dot(w2[at, :grades], dproj_t[...], preferred_element_type=F32)
         dpre_t[n * hb : (n + 1) * hb, :] = jnp.where(mask_t[at, :] > 0, d, 0.0).astype(BF16)
 
     orders = stage_bits(parts, fsize)
@@ -270,22 +385,30 @@
                 elif t + 1 < stages:
                     acc[c, k[0], k[1]] = new
                 else:
-                    grad_t[:, c * half : (c + 1) * half] = new
+                    grad_out[c * half : (c + 1) * half, :] = new.T
             if t + 1 < stages:
                 flying[c] = launch(c, t + 1)
         for _, _, r in smalls:
             r.wait()
         for f, slot, _ in smalls:
             sm[f] = sm[f] + smin[slot]
-    small_out[...] = sm[0]
-
-
-def later(dims, agg, w1, b1, w2, tiles, src, live, table, labels):
-    parts, fsize, slots, nblocks, per_block, blk, grades, scale = dims
+    bias_out[...] = sm[0, grades : grades + 1, :]
+    second_out[...] = sm[0, :grades, :].T
+
+
+def shards(features, pair_count, send_blocks, tile_src, tiles, labels, w_first, b_first, w_second):
+    nodes, fw = features.shape
+    nblocks, per_block = tile_src.shape
+    blk = tiles.shape[2]
+    parts = lax.axis_size("nodes")
+    fsize = lax.axis_size("feat")
+    slots = send_blocks.shape[2]
+    grades = w_second.shape[1]
     mine = nblocks // fsize
-    rows, feats = agg.shape
-    hid = w1.shape[1]
-    fw, hb = feats // fsize, hid // parts
+    rows, feats, hid = nodes // fsize, fw * fsize, w_first.shape[1]
+    hb = hid // parts
+    half = fw // 2
+    dims = (parts, fsize, slots, nblocks, per_block, blk, grades, 1.0 / math.sqrt(nodes * parts))
     stages = len(stage_bits(parts, fsize)[0])
     tiles_sent = fsize * parts - 1
     n_small = (fsize - 1) + (parts.bit_length() - 1)
@@ -293,15 +416,26 @@
     sc = pl.BlockSpec(memory_space=pltpu.SMEM)
     dma = pltpu.SemaphoreType.DMA
     field = (grades, blk)
-    return pl.pallas_call(
-        functools.partial(later_kernel, dims),
+    grad_first, grad_bias, grad_second = pl.pallas_call(
+        functools.partial(whole_kernel, dims),
         out_shape=(
-            jax.ShapeDtypeStruct((hb, fw), F32),
-            jax.ShapeDtypeStruct((grades + 8, fw), F32),
+            jax.ShapeDtypeStruct((fw, hb), F32),
+            jax.ShapeDtypeStruct((1, fw), F32),
+            jax.ShapeDtypeStruct((fw, grades), F32),
         ),
-        in_specs=[vm, vm, vm, vm, vm, pl.BlockSpec(memory_space=pl.ANY), sc, sc, sc, vm],
-        out_specs=(vm, vm),
+        in_specs=[vm, vm, vm, vm, pl.BlockSpec(memory_space=pl.ANY), sc, sc, sc, vm],
+        out_specs=(vm, vm, vm),
         scratch_shapes=[
+            pltpu.VMEM((rows, feats), BF16),
+            pltpu.VMEM((feats, hid), BF16),
+            pltpu.VMEM((hid, blk), BF16),
+            pltpu.VMEM((fsize, 8, fw), F32),
+            pltpu.VMEM((grades, hid), BF16),
+            pltpu.VMEM((1, hid), F32),
+            pltpu.VMEM((2, parts, slots, blk, half), BF16),
+            pltpu.VMEM((parts, slots, blk, half), BF16),
+            pltpu.VMEM((parts, slots, blk, half), BF16),
+            pltpu.VMEM((2, nodes, half), BF16),
             pltpu.VMEM((rows, hid), BF16),
             pltpu.VMEM((hid, rows), BF16),
             pltpu.VMEM((rows, hid), BF16),
@@ -309,7 +443,7 @@
             pltpu.VMEM((parts, slots) + field, F32),
             pltpu.VMEM((parts, slots) + field, F32),
             pltpu.VMEM((parts * slots, 3 * grades, blk), BF16),
-            pltpu.VMEM((mine, per_block, blk, blk), BF16),
+            pltpu.VMEM((nblocks, per_block, blk, blk), BF16),
             pltpu.VMEM((mine,) + field, F32),
             pltpu.VMEM((mine * per_block,) + field, F32),
             pltpu.VMEM((parts, slots) + field, F32),
@@ -318,12 +452,17 @@
             pltpu.VMEM((fsize - 1, mine) + field, F32),
             pltpu.VMEM((grades, rows), BF16),
             pltpu.VMEM((hid, rows), BF16),
-            pltpu.VMEM((2, fsize, parts, hb, fw // 2), F32),
-            pltpu.VMEM((2, tiles_sent, hb, fw // 2), BF16),
-            pltpu.VMEM((2, tiles_sent, hb, fw // 2), BF16),
+            pltpu.VMEM((2, fsize, parts, hb, half), F32),
+            pltpu.VMEM((2, tiles_sent, hb, half), BF16),
+            pltpu.VMEM((2, tiles_sent, hb, half), BF16),
             pltpu.VMEM((fsize, grades + 8, fw), F32),
             pltpu.VMEM((n_small, grades + 8, fw), F32),
             dma,
+            dma((fsize,)), dma((fsize,)),
+            dma((fsize,)), dma((fsize,)),
+            dma((fsize,)), dma((fsize,)),
+            dma((2, parts)), dma((2, parts)),
+            dma((2, fsize)), dma((2, fsize)),
             dma((fsize,)), dma((fsize,)),
             dma((parts,)), dma((parts,)),
             dma((parts,)), dma((parts,)),
@@ -332,43 +471,16 @@
             dma((n_small,)), dma((n_small,)),
         ],
         compiler_params=pltpu.CompilerParams(
-            collective_id=1, has_side_effects=True, vmem_limit_bytes=56 * 1024 * 1024
+            collective_id=1, has_side_effects=True, vmem_limit_bytes=60 * 1024 * 1024
         ),
         cost_estimate=pl.CostEstimate(
             flops=4 * rows * hid * feats, bytes_accessed=6 * rows * hid, transcendentals=rows * grades
         ),
-    )(agg, w1, b1, w2, w2.T, tiles, src, live, table, labels)
-
-
-def shards(features, pair_count, send_blocks, tile_src, tiles, labels, w_first, b_first, w_second):
-    rows, width = features.shape
-    nblocks, per_block = tile_src.shape
-    blk = tiles.shape[2]
-    parts = lax.axis_size("nodes")
-    fsize = lax.axis_size("feat")
-    slots = send_blocks.shape[2]
-    grades = w_second.shape[1]
-    live = (tile_src % slots) < pair_count[0][tile_src // slots]
-    weights = tiles * live[:, :, None, None].astype(BF16)
-    table = send_blocks[0]
-
-    w1 = lax.all_gather(w_first, "feat", axis=0, tiled=True)
-    w2 = lax.all_gather(w_second, "feat", axis=0, tiled=True)
-    b1 = lax.all_gather(b_first, "feat", axis=0, tiled=True)
-
-    own_one = features.reshape(nblocks, blk, width)
-    arrived = lax.all_to_all(own_one[table], "nodes", split_axis=0, concat_axis=0, tiled=True)
-    sources = arrived.reshape(parts * slots, blk, width)[tile_src]
-    summed = jnp.einsum("btij,btjf->bif", weights, sources, preferred_element_type=F32)
-    agg = (summed + own_one).astype(BF16).reshape(rows, width)
-    agg = lax.all_to_all(agg, "feat", split_axis=0, concat_axis=1, tiled=True)
-
-    dims = (parts, fsize, slots, nblocks, per_block, blk, grades, 1.0 / math.sqrt(rows * parts))
-    grad_t, small = later(
-        dims, agg, w1, b1[None, :], w2, tiles, tile_src, live.astype(F32), table,
-        labels.reshape(nblocks, blk),
+    )(
+        features.reshape(nblocks, blk, fw), w_first, b_first[None, :], w_second, tiles, tile_src,
+        pair_count, send_blocks, labels.reshape(nblocks, blk),
     )
-    return (grad_t.T, small[grades], small[:grades].T)
+    return (grad_first, grad_bias[0], grad_second)
 
 
 def solution(mesh):

time: 166 us -> 112 us (0.67)
  Pallas kernels: 56.2 us -> 102 us
  blocking collectives: 32.2 us -> 0 us
  waiting for transfers between devices: 23.3 us -> 0 us
  between operations: 14.1 us -> 0.64 us
  starting transfers between devices: 11.1 us -> 0 us
  local copies, waits for them, and re-layouts: 19.1 us -> 8.52 us
  matrix products: 7.82 us -> 0 us
    pallas_call x1, Pallas kernels: 56.2 us -> 102 us  [shards(): pl.pallas_call(functools.partial(whole_kernel, dims), out_shape=(jax.Shap...]
    all_gather x2 -> x0, blocking collectives: 32.2 us -> none  [the longest x1 26.7 us: shards(): w2 = lax.all_gather(w_second, 'feat', axis=0, tiled=True)]
    all_to_all x2 -> x0, waiting for transfers between devices: 22.6 us -> none  [the longest x1 22.6 us: shards(): lax.all_to_all(own_one[table], 'nodes', split_axis=0, concat_axis=0, tile...]
    gather x4 -> x0, local copies, waits for them, and re-layouts: 11.1 us -> none  [the longest x1 6.57 us: shards(): sources = arrived.reshape(parts * slots, blk, width)[tile_src]]
    all_to_all x2 -> x0, starting transfers between devices: 11 us -> none  [the longest x1 7.28 us: shards(): lax.all_to_all(own_one[table], 'nodes', split_axis=0, concat_axis=0, tile...]
    dot_general x1 -> x0, matrix products: 7.82 us -> none  [shards(): jnp.einsum('btij,btjf->bif', weights, sources, preferred_element_type=F32)]
    unnamed x18 -> x6, local copies, waits for them, and re-layouts: 1.78 us -> 8.52 us
  transfers between devices with their start and end apart: 3 -> 0, of which waited for: 1 -> 0; matrix products, arithmetic and copies ran while one was open for 12% -> 0% of each run, Pallas kernels for 0% -> 0%
where the time goes in v3:
time: 112 us; the launch traced here: 111 us
  Pallas kernels  102 us (91%)
  local copies, waits for them, and re-layouts  8.52 us (8%)
    pallas_call x1, Pallas kernels, shards(): pl.pallas_call(functools.partial(whole_kernel, dims), out_shape=(jax.Shap...  102 us
    unnamed x6, local copies, waits for them, and re-layouts  8.52 us

profile of v3, /device:TPU:0, one launch (start us, length us, event | category | flops | bytes accessed | tf_op | source)
XLA Modules:
  0.0 111.2 jit_solution(15677072681631548247)
XLA Ops:
  0.6 1.3 %copy.14.table = s32[1,8,2]{2,1,0:T(8,128)} copy(s32[1,8,2]{1,2,0:T(2,128)} %param.11) | data formatting | bytes 128 | tf_op args[2]
  2.0 1.4 %copy.13.src = s32[32,4]{1,0:T(8,128)} copy(s32[32,4]{0,1:T(4,128)} %param.12) | data formatting | bytes 1024 | tf_op args[3]
  3.3 1.4 %copy.12.w2_in = bf16[256,16]{1,0:T(8,128)(2,1)} copy(bf16[256,16]{0,1:T(8,128)(2,1)} %param.17) | data formatting | bytes 16384 | tf_op args[8]
  4.8 102.1 %shard_map.112 = (f32[256,128]{1,0:T(8,128)}, f32[1,256]{1,0:T(1,128)}, f32[256,16]{1,0:T(8,128)}) custom-call(bf16[32,128,256]{2,1,0:T(8,128)(2,1)} %bitcast.5, bf16[256,1024]{1,0:T(8,128)(2,1)} %w_in.1, f32[1,256]{1,0:T(1,128)} %bitcast.7, bf16[256,16]{1,0:T(8,128)(2,1)} %copy.12.w2_in, bf16[32,4,128,128]{3,2,1,0:T(8,128)(2,1)} %tiles.1, ...), custom_call_target="tpu_custom_call" | custom-call | flops 4294967296 | bytes 6291456 | tf_op jit(solution)/shard_map/pallas_call | solution.py:419
  106.9 1.6 %copy.15 = f32[256,16]{0,1:T(8,128)} copy(f32[256,16]{1,0:T(8,128)} %get-tuple-element.11) | data formatting | bytes 32768
  108.5 1.6 %copy.18 = f32[256,128]{1,0:T(8,128)} copy(f32[256,128]{1,0:T(8,128)} %get-tuple-element.15) | data formatting | bytes 262144
  110.0 1.2 %copy.19 = f32[256]{0:T(256)} copy(f32[256]{0:T(256)} %bitcast.4) | data formatting | bytes 2048

commit v4 on v3

--- a/solution.py
+++ b/solution.py
@@ -52,9 +52,9 @@
 
 
 def whole_kernel(
-    dims, feats_in, w_in, b_in, w2_in, tiles, src, count, table, labels, grad_out, bias_out, second_out,
-    agg, w1, w2, b_all, w2t, b1, fsend, frecv_a, frecv_b, abuf,
-    mask, mask_t, hidden, pall, sbuf, rbuf, r3, tl, dl, contrib, sback, rback, spread, rspread,
+    dims, feats_in, w_in, b_in, w2t_in, tiles, src, count, table, labels, grad_out, bias_out, second_out,
+    agg, w1, w2, w2_all, b_all, w2t, b1, fsend, frecv_a, frecv_b, abuf,
+    part, mask, mask_t, hidden, pall, sbuf, rbuf, r3, tl, dl, contrib, sback, rback, spread, rspread,
     dproj_t, dpre_t, acc, gout, gin, sm, smin, tile_sem,
     w_s, w_r, w2_s, w2_r, b_s, b_r, fx_s, fx_r, tr_s, tr_r,
     ag_s, ag_r, ex_s, ex_r, bk_s, bk_r, sp_s, sp_r, rs_s, rs_r, sm_s, sm_r,
@@ -70,7 +70,7 @@
     base = me_f * mine
 
     def live(b, k):
-        slot = src[b, k]
+        slot = src[k, b]
         return jnp.where(slot % slots < count[0, slot // slots], 1.0, 0.0)
 
     fetch = pltpu.make_async_copy(tiles, tl, tile_sem)
@@ -78,8 +78,7 @@
     frecv = (frecv_a, frecv_b)
     own_w = pl.ds(pl.multiple_of(me_f * fw, fw), fw)
     w1[own_w, :] = w_in[...]
-    w2[own_w, :] = jnp.zeros((fw, blk), BF16)
-    w2[own_w, :grades] = w2_in[...]
+    w2_all[me_f] = w2t_in[...]
     b_all[me_f] = jnp.broadcast_to(b_in[...], (8, fw))
     greet(parts, fsize, me_n, me_f)
 
@@ -91,7 +90,7 @@
         return remote(fsend.at[c, p], frecv[c].at[me_n], fx_s.at[c, d], fx_r.at[c, d], (p, me_f))
 
     def stage_block(c, p, s):
-        fsend[c, p, s] = feats_in[table[0, p, s], :, column(c)]
+        fsend[c, p, s] = feats_in[table[s, p], :, column(c)]
 
     for p in range(parts):
         for s in range(slots):
@@ -115,7 +114,7 @@
             (far if j > 1 else weights_flying).append(x)
     for d in range(1, fsize):
         to = (me_n, (me_f + d) % fsize)
-        x = remote(w2.at[own_w, :], w2.at[own_w, :], w2_s.at[d], w2_r.at[d], to)
+        x = remote(w2_all.at[me_f], w2_all.at[me_f], w2_s.at[d], w2_r.at[d], to)
         x.start()
         y = remote(b_all.at[me_f], b_all.at[me_f], b_s.at[d], b_r.at[d], to)
         y.start()
@@ -142,7 +141,7 @@
         def block(b):
             wcat = jnp.concatenate([tl[b, k] * live(b, k).astype(BF16) for k in range(per_block)], axis=1)
             got = jnp.concatenate(
-                [frecv[c][src[b, k] // slots, src[b, k] % slots] for k in range(per_block)], axis=0
+                [frecv[c][src[k, b] // slots, src[k, b] % slots] for k in range(per_block)], axis=0
             )
             total = jnp.dot(wcat, got, preferred_element_type=F32)
             return (total + feats_in[b, :, column(c)].astype(F32)).astype(BF16)
@@ -152,13 +151,15 @@
         for j in order:
             group = flip(me_f, j)
 
-            @pl.loop(0, mine)
-            def _(i):
-                got = block(group * mine + i)
-                if j:
-                    abuf[c, pl.ds(pl.multiple_of((group * mine + i) * blk, blk), blk), :] = got
-                else:
-                    agg[pl.ds(pl.multiple_of(i * blk, blk), blk), lanes] = got
+            @pl.loop(0, mine // 4)
+            def _(r):
+                done = [block(group * mine + r * 4 + i) for i in range(4)]
+                for i, got in enumerate(done):
+                    if j:
+                        to = pl.multiple_of((group * mine + r * 4 + i) * blk, blk)
+                        abuf[c, pl.ds(to, blk), :] = got
+                    else:
+                        agg[pl.ds(pl.multiple_of((r * 4 + i) * blk, blk), blk), lanes] = got
 
             if j:
                 at = pl.ds(pl.multiple_of(group * rows, rows), rows)
@@ -167,7 +168,7 @@
                 sent.append(x)
         return sent
 
-    turned = aggregate(0)
+    turned_a = aggregate(0)
     for x in far:
         x.wait()
     for j in range(3, fsize):
@@ -178,19 +179,33 @@
             weights_flying.append(x)
     for x in second:
         x.wait()
-    turned += aggregate(1)
+    turned_b = aggregate(1)
     for x in weights_flying:
         x.wait()
     for f in range(fsize):
         b1[:, f * fw : (f + 1) * fw] = b_all[f, :1, :]
-    w2t[...] = w2[...].T[:grades]
-    for x in turned:
+        w2t[:, f * fw : (f + 1) * fw] = w2_all[f]
+    def depth_half(c, at):
+        lhs = jnp.concatenate([agg[at, f * fw + c * half : f * fw + (c + 1) * half] for f in range(fsize)], axis=1)
+        rhs = jnp.concatenate([w1[f * fw + c * half : f * fw + (c + 1) * half, :] for f in range(fsize)], axis=0)
+        return jnp.dot(lhs, rhs, preferred_element_type=F32)
+
+    for x in turned_a:
         x.wait()
 
     @pl.loop(0, 4)
     def _(r):
         at = pl.ds(pl.multiple_of(r * width, width), width)
-        pre = jnp.dot(agg[at, :], w1[...], preferred_element_type=F32) + b1[...]
+        part[at, :] = depth_half(0, at)
+
+    w2[...] = jnp.concatenate([w2t[...], jnp.zeros((blk - grades, hid), BF16)], axis=0).T
+    for x in turned_b:
+        x.wait()
+
+    @pl.loop(0, 4)
+    def _(r):
+        at = pl.ds(pl.multiple_of(r * width, width), width)
+        pre = part[at, :] + depth_half(1, at) + b1[...]
         hb16 = jnp.maximum(pre, 0.0).astype(BF16)
         hidden[at, :] = hb16
         mask[at, :] = jnp.where(pre > 0, 1.0, 0.0).astype(BF16)
@@ -214,7 +229,7 @@
         c.wait()
     for p in range(parts):
         for s in range(slots):
-            sbuf[p, s] = pall[table[0, p, s]]
+            sbuf[p, s] = pall[table[s, p]]
     rbuf[me_n] = sbuf[me_n]
     copies = []
     for d in range(1, parts):
@@ -235,23 +250,34 @@
 
     grade_id = lax.broadcasted_iota(jnp.int32, (grades, blk), 0)
 
-    @pl.loop(0, mine)
-    def _(b):
-        pieces = [r3[src[base + b, k]] * live(base + b, k).astype(BF16) for k in range(per_block)]
-        lhs = jnp.concatenate(pieces, axis=1)
-        wcat = jnp.concatenate([tl[base + b, k] for k in range(per_block)], axis=1)
-        out = lax.dot_general(lhs, wcat, (((1,), (1,)), ((), ())), preferred_element_type=F32)
-        logits = pall[base + b] + (
-            out[:grades] + (out[grades : 2 * grades] + out[2 * grades : 3 * grades])
-        )
-        expo = jnp.exp(logits)
-        probs = expo / jnp.sum(expo, axis=0, keepdims=True)
-        onehot = jnp.where(labels[pl.ds(base + b, 1), :] == grade_id, 1.0, 0.0)
-        dlog = (probs - onehot) * scale
-        dl[b] = dlog
-        back = jnp.dot(dlog.astype(BF16), wcat, preferred_element_type=F32)
-        for k in range(per_block):
-            contrib[b * per_block + k] = back[:, k * blk : (k + 1) * blk] * live(base + b, k)
+    @pl.loop(0, mine // 4)
+    def _(r):
+        four = [r * 4 + i for i in range(4)]
+        wcats, outs = [], []
+        for b in four:
+            pieces = [r3[src[k, base + b]] * live(base + b, k).astype(BF16) for k in range(per_block)]
+            lhs = jnp.concatenate(pieces, axis=1)
+            wcats.append(jnp.concatenate([tl[base + b, k] for k in range(per_block)], axis=1))
+            outs.append(
+                lax.dot_general(lhs, wcats[-1], (((1,), (1,)), ((), ())), preferred_element_type=F32)
+            )
+        dlogs = []
+        for b, out in zip(four, outs):
+            logits = pall[base + b] + (
+                out[:grades] + (out[grades : 2 * grades] + out[2 * grades : 3 * grades])
+            )
+            expo = jnp.exp(logits)
+            probs = expo / jnp.sum(expo, axis=0, keepdims=True)
+            onehot = jnp.where(labels[pl.ds(base + b, 1), :] == grade_id, 1.0, 0.0)
+            dlogs.append((probs - onehot) * scale)
+        backs = [
+            jnp.dot(dlog.astype(BF16), wcat, preferred_element_type=F32)
+            for dlog, wcat in zip(dlogs, wcats)
+        ]
+        for b, dlog, back in zip(four, dlogs, backs):
+            dl[b] = dlog
+            for k in range(per_block):
+                contrib[b * per_block + k] = back[:, k * blk : (k + 1) * blk] * live(base + b, k)
 
     @pl.loop(0, parts)
     def _(p):
@@ -260,9 +286,9 @@
             total = jnp.zeros((grades, blk), F32)
             for b in range(mine):
                 for k in range(per_block):
-                    hit = jnp.where(src[base + b, k] == slot, 1.0, 0.0)
+                    hit = jnp.where(src[k, base + b] == slot, 1.0, 0.0)
                     total = total + contrib[b * per_block + k] * hit
-            sback[p, s] = total
+            sback[p, s] = total.astype(BF16)
 
     rback[me_n] = sback[me_n]
     copies = []
@@ -274,14 +300,14 @@
     for c in copies:
         c.wait()
 
+    came = [(rback[p, s].astype(F32), p, s) for p in range(parts) for s in range(slots)]
+
     @pl.loop(0, nblocks)
     def _(b):
         total = jnp.zeros((grades, blk), F32)
-        for p in range(parts):
-            for s in range(slots):
-                hit = jnp.where(table[0, p, s] == b, 1.0, 0.0)
-                total = total + rback[p, s] * hit
-        spread[b] = total
+        for x, p, s in came:
+            total = total + x * jnp.where(table[s, p] == b, 1.0, 0.0)
+        spread[b] = total.astype(BF16)
 
     copies = []
     for d in range(1, fsize):
@@ -294,9 +320,9 @@
     for c in copies:
         c.wait()
     for b in range(mine):
-        total = spread[base + b]
+        total = spread[base + b].astype(F32)
         for d in range(fsize - 1):
-            total = total + rspread[d, b]
+            total = total + rspread[d, b].astype(F32)
         dproj_t[:, b * blk : (b + 1) * blk] = (dl[b] + total).astype(BF16)
 
     for n in range(parts):
@@ -393,7 +419,7 @@
         for f, slot, _ in smalls:
             sm[f] = sm[f] + smin[slot]
     bias_out[...] = sm[0, grades : grades + 1, :]
-    second_out[...] = sm[0, :grades, :].T
+    second_out[...] = sm[0, :grades, :]
 
 
 def shards(features, pair_count, send_blocks, tile_src, tiles, labels, w_first, b_first, w_second):
@@ -421,7 +447,7 @@
         out_shape=(
             jax.ShapeDtypeStruct((fw, hb), F32),
             jax.ShapeDtypeStruct((1, fw), F32),
-            jax.ShapeDtypeStruct((fw, grades), F32),
+            jax.ShapeDtypeStruct((grades, fw), F32),
         ),
         in_specs=[vm, vm, vm, vm, pl.BlockSpec(memory_space=pl.ANY), sc, sc, sc, vm],
         out_specs=(vm, vm, vm),
@@ -429,6 +455,7 @@
             pltpu.VMEM((rows, feats), BF16),
             pltpu.VMEM((feats, hid), BF16),
             pltpu.VMEM((hid, blk), BF16),
+            pltpu.VMEM((fsize, grades, fw), BF16),
             pltpu.VMEM((fsize, 8, fw), F32),
             pltpu.VMEM((grades, hid), BF16),
             pltpu.VMEM((1, hid), F32),
@@ -436,6 +463,7 @@
             pltpu.VMEM((parts, slots, blk, half), BF16),
             pltpu.VMEM((parts, slots, blk, half), BF16),
             pltpu.VMEM((2, nodes, half), BF16),
+            pltpu.VMEM((rows, hid), F32),
             pltpu.VMEM((rows, hid), BF16),
             pltpu.VMEM((hid, rows), BF16),
             pltpu.VMEM((rows, hid), BF16),
@@ -446,10 +474,10 @@
             pltpu.VMEM((nblocks, per_block, blk, blk), BF16),
             pltpu.VMEM((mine,) + field, F32),
             pltpu.VMEM((mine * per_block,) + field, F32),
-            pltpu.VMEM((parts, slots) + field, F32),
-            pltpu.VMEM((parts, slots) + field, F32),
-            pltpu.VMEM((nblocks,) + field, F32),
-            pltpu.VMEM((fsize - 1, mine) + field, F32),
+            pltpu.VMEM((parts, slots) + field, BF16),
+            pltpu.VMEM((parts, slots) + field, BF16),
+            pltpu.VMEM((nblocks,) + field, BF16),
+            pltpu.VMEM((fsize - 1, mine) + field, BF16),
             pltpu.VMEM((grades, rows), BF16),
             pltpu.VMEM((hid, rows), BF16),
             pltpu.VMEM((2, fsize, parts, hb, half), F32),
@@ -477,10 +505,10 @@
             flops=4 * rows * hid * feats, bytes_accessed=6 * rows * hid, transcendentals=rows * grades
         ),
     )(
-        features.reshape(nblocks, blk, fw), w_first, b_first[None, :], w_second, tiles, tile_src,
-        pair_count, send_blocks, labels.reshape(nblocks, blk),
+        features.reshape(nblocks, blk, fw), w_first, b_first[None, :], w_second.T, tiles, tile_src.T,
+        pair_count, send_blocks[0].T, labels.reshape(nblocks, blk),
     )
-    return (grad_first, grad_bias[0], grad_second)
+    return (grad_first, grad_bias[0], grad_second.T)
 
 
 def solution(mesh):

time: 112 us -> 102 us (0.911)
  Pallas kernels: 102 us -> 97 us
  local copies, waits for them, and re-layouts: 8.52 us -> 4.11 us
    pallas_call x1, Pallas kernels: 102 us -> 97 us  [shards(): pl.pallas_call(functools.partial(whole_kernel, dims), out_shape=(jax.Shap...]
    unnamed x6 -> x3, local copies, waits for them, and re-layouts: 8.52 us -> 4.11 us
where the time goes in v4:
time: 102 us
  Pallas kernels  97 us (95%)
  local copies, waits for them, and re-layouts  4.11 us (4%)
    pallas_call x1, Pallas kernels, shards(): pl.pallas_call(functools.partial(whole_kernel, dims), out_shape=(jax.Shap...  97 us
    unnamed x3, local copies, waits for them, and re-layouts  4.11 us

profile of v4, /device:TPU:0, one launch (start us, length us, event | category | flops | bytes accessed | tf_op | source)
XLA Modules:
  0.0 101.8 jit_solution(13902659069287250693)
XLA Ops:
  0.6 97.0 %shard_map.112 = (f32[256,128]{1,0:T(8,128)}, f32[1,256]{1,0:T(1,128)}, f32[16,256]{1,0:T(8,128)}) custom-call(bf16[32,128,256]{2,1,0:T(8,128)(2,1)} %bitcast.12, bf16[256,1024]{1,0:T(8,128)(2,1)} %w_in.1, f32[1,256]{1,0:T(1,128)} %bitcast.16, bf16[16,256]{1,0:T(8,128)(2,1)} %bitcast.14, bf16[32,4,128,128]{3,2,1,0:T(8,128)(2,1)} %tiles.1, s32[4,32]{1,0:T(4,128)} %bitcast.15, ...), custom_call_target="tpu_custom_call" | custom-call | flops 4294967296 | bytes 6291456 | tf_op jit(solution)/shard_map/pallas_call | solution.py:445
  97.7 1.6 %copy.15 = f32[256,128]{1,0:T(8,128)} copy(f32[256,128]{1,0:T(8,128)} %get-tuple-element.12) | data formatting | bytes 262144
  99.2 1.2 %copy.16 = f32[256]{0:T(256)} copy(f32[256]{0:T(256)} %bitcast.11) | data formatting | bytes 2048
  100.4 1.3 %copy.17 = f32[256,16]{0,1:T(8,128)} copy(f32[256,16]{0,1:T(8,128)} %bitcast.10) | data formatting | bytes 32768

commit v5 on v4

--- a/solution.py
+++ b/solution.py
@@ -28,7 +28,7 @@
         pl.semaphore_signal(barrier, inc=1, device_id=(me_n, (me_f + d) % fsize), device_id_type=MESH)
     for d in range(1, parts):
         pl.semaphore_signal(barrier, inc=1, device_id=((me_n + d) % parts, me_f), device_id_type=MESH)
-    pl.semaphore_wait(barrier, fsize + parts - 2)
+    return barrier
 
 
 def remote(src, dst, send, recv, device):
@@ -52,12 +52,12 @@
 
 
 def whole_kernel(
-    dims, feats_in, w_in, b_in, w2t_in, tiles, src, count, table, labels, grad_out, bias_out, second_out,
-    agg, w1, w2, w2_all, b_all, w2t, b1, fsend, frecv_a, frecv_b, abuf,
+    dims, feats_hbm, w_hbm, b_in, w2t_in, tiles, src, count, table, labels, grad_out, bias_out, second_out,
+    feats_in, agg, w1, w2, w2_all, b_all, w2t, b1, fsend, frecv_a, frecv_b, abuf,
     part, mask, mask_t, hidden, pall, sbuf, rbuf, r3, tl, dl, contrib, sback, rback, spread, rspread,
-    dproj_t, dpre_t, acc, gout, gin, sm, smin, tile_sem,
+    dproj_t, dpre_t, acc, gout, gin, sm, smin, tile_sem, feat_sem, w_sem,
     w_s, w_r, w2_s, w2_r, b_s, b_r, fx_s, fx_r, tr_s, tr_r,
-    ag_s, ag_r, ex_s, ex_r, bk_s, bk_r, sp_s, sp_r, rs_s, rs_r, sm_s, sm_r,
+    ag_s, ag_r, ex_s, ex_r, bk_s, bk_r, sp_s, sp_r, z_s, z_r, rs_s, rs_r, sm_s, sm_r,
 ):
     parts, fsize, slots, nblocks, per_block, blk, grades, scale = dims
     me_n, me_f = lax.axis_index("nodes"), lax.axis_index("feat")
@@ -73,14 +73,17 @@
         slot = src[k, b]
         return jnp.where(slot % slots < count[0, slot // slots], 1.0, 0.0)
 
+    barrier = greet(parts, fsize, me_n, me_f)
+    frecv = (frecv_a, frecv_b)
+    own_w = pl.ds(pl.multiple_of(me_f * fw, fw), fw)
+    fetch_feats = pltpu.make_async_copy(feats_hbm, feats_in, feat_sem)
+    fetch_feats.start()
+    fetch_w = pltpu.make_async_copy(w_hbm, w1.at[own_w, :], w_sem)
+    fetch_w.start()
     fetch = pltpu.make_async_copy(tiles, tl, tile_sem)
     fetch.start()
-    frecv = (frecv_a, frecv_b)
-    own_w = pl.ds(pl.multiple_of(me_f * fw, fw), fw)
-    w1[own_w, :] = w_in[...]
     w2_all[me_f] = w2t_in[...]
     b_all[me_f] = jnp.broadcast_to(b_in[...], (8, fw))
-    greet(parts, fsize, me_n, me_f)
 
     def column(c):
         return slice(c * half, (c + 1) * half)
@@ -92,9 +95,11 @@
     def stage_block(c, p, s):
         fsend[c, p, s] = feats_in[table[s, p], :, column(c)]
 
+    fetch_feats.wait()
     for p in range(parts):
         for s in range(slots):
             stage_block(0, p, s)
+    pl.semaphore_wait(barrier, fsize + parts - 2)
     first = []
     for d in range(1, parts):
         x = exchange(0, d)
@@ -107,6 +112,7 @@
 
     weights_flying = []
     far = []
+    fetch_w.wait()
     for j in range(1, fsize):
         if j & (j - 1) == 0:
             x = pass_on(0, j, j)
@@ -202,23 +208,22 @@
     for x in turned_b:
         x.wait()
 
-    @pl.loop(0, 4)
-    def _(r):
-        at = pl.ds(pl.multiple_of(r * width, width), width)
+    copies = []
+    per = width // blk
+    for r in range(4):
+        at = slice(r * width, (r + 1) * width)
         pre = part[at, :] + depth_half(1, at) + b1[...]
         hb16 = jnp.maximum(pre, 0.0).astype(BF16)
         hidden[at, :] = hb16
         mask[at, :] = jnp.where(pre > 0, 1.0, 0.0).astype(BF16)
         pt = lax.dot_general(w2t[...], hb16, (((1,), (1,)), ((), ())), preferred_element_type=F32)
-        for i in range(width // blk):
-            pall[base + r * (width // blk) + i] = pt[:, i * blk : (i + 1) * blk]
-
-    copies = []
-    for d in range(1, fsize):
-        own = pall.at[pl.ds(base, mine)]
-        c = remote(own, own, ag_s.at[d], ag_r.at[d], (me_n, (me_f + d) % fsize))
-        c.start()
-        copies.append(c)
+        for i in range(per):
+            pall[base + r * per + i] = pt[:, i * blk : (i + 1) * blk]
+        for d in range(1, fsize):
+            own = pall.at[pl.ds(base + r * per, per)]
+            c = remote(own, own, ag_s.at[r, d], ag_r.at[r, d], (me_n, (me_f + d) % fsize))
+            c.start()
+            copies.append(c)
 
     @pl.loop(0, 4)
     def _(r):
@@ -352,16 +357,17 @@
         axis, bit = orders[c][t]
         return [j for j in kept(orders[c], t, fsize, parts) if (j[0] if axis == "f" else j[1]) & bit]
 
-    flying = [None, None]
-    for f in range(fsize):
-        if f & 1:
-            g = product(f).astype(BF16)
-            for c in range(2):
-                for i, j in enumerate(going(c, 0)):
-                    if j[0] == f:
-                        gout[c, i] = g[j[1] * hb : (j[1] + 1) * hb, c * half : (c + 1) * half]
-    for c in range(2):
-        flying[c] = launch(c, 0)
+    flying = [[], []]
+    for f in range(fsize - 1, 0, -2):
+        g = product(f).astype(BF16)
+        for c in range(2):
+            first_tile = (f // 2) * parts
+            for n in range(parts):
+                gout[c, first_tile + n] = g[n * hb : (n + 1) * hb, c * half : (c + 1) * half]
+            at = pl.ds(first_tile, parts)
+            r = remote(gout.at[c, at], gin.at[c, at], z_s.at[c, f], z_r.at[c, f], partner("f", 1))
+            r.start()
+            flying[c].append(r)
     for f in range(fsize):
         if not f & 1:
             g = product(f)
@@ -399,7 +405,8 @@
             smalls.append((f - bit if axis == "f" else 0, at_small, r))
             at_small += 1
         for c in range(2):
-            flying[c].wait()
+            for r in flying[c]:
+                r.wait()
             sent = going(c, t)
             axis_c, bit_c = orders[c][t]
             for i, j in enumerate(sent):
@@ -413,13 +420,19 @@
                 else:
                     grad_out[c * half : (c + 1) * half, :] = new.T
             if t + 1 < stages:
-                flying[c] = launch(c, t + 1)
+                flying[c] = [launch(c, t + 1)]
         for _, _, r in smalls:
             r.wait()
         for f, slot, _ in smalls:
             sm[f] = sm[f] + smin[slot]
     bias_out[...] = sm[0, grades : grades + 1, :]
     second_out[...] = sm[0, :grades, :]
+
+
+def hand_over(a, b, c, a_out, b_out, c_out):
+    a_out[...] = a[...]
+    b_out[...] = b[...]
+    c_out[...] = c[...]
 
 
 def shards(features, pair_count, send_blocks, tile_src, tiles, labels, w_first, b_first, w_second):
@@ -440,6 +453,7 @@
     n_small = (fsize - 1) + (parts.bit_length() - 1)
     vm = pl.BlockSpec(memory_space=pltpu.VMEM)
     sc = pl.BlockSpec(memory_space=pltpu.SMEM)
+    hbm = pl.BlockSpec(memory_space=pl.ANY)
     dma = pltpu.SemaphoreType.DMA
     field = (grades, blk)
     grad_first, grad_bias, grad_second = pl.pallas_call(
@@ -449,9 +463,10 @@
             jax.ShapeDtypeStruct((1, fw), F32),
             jax.ShapeDtypeStruct((grades, fw), F32),
         ),
-        in_specs=[vm, vm, vm, vm, pl.BlockSpec(memory_space=pl.ANY), sc, sc, sc, vm],
+        in_specs=[hbm, hbm, vm, vm, hbm, sc, sc, sc, vm],
         out_specs=(vm, vm, vm),
         scratch_shapes=[
+            pltpu.VMEM((nblocks, blk, fw), BF16),
             pltpu.VMEM((rows, feats), BF16),
             pltpu.VMEM((feats, hid), BF16),
             pltpu.VMEM((hid, blk), BF16),
@@ -486,15 +501,18 @@
             pltpu.VMEM((fsize, grades + 8, fw), F32),
             pltpu.VMEM((n_small, grades + 8, fw), F32),
             dma,
+            dma,
+            dma,
             dma((fsize,)), dma((fsize,)),
             dma((fsize,)), dma((fsize,)),
             dma((fsize,)), dma((fsize,)),
             dma((2, parts)), dma((2, parts)),
             dma((2, fsize)), dma((2, fsize)),
-            dma((fsize,)), dma((fsize,)),
+            dma((4, fsize)), dma((4, fsize)),
             dma((parts,)), dma((parts,)),
             dma((parts,)), dma((parts,)),
             dma((fsize,)), dma((fsize,)),
+            dma((2, fsize)), dma((2, fsize)),
             dma((2, stages)), dma((2, stages)),
             dma((n_small,)), dma((n_small,)),
         ],
@@ -508,6 +526,12 @@
         features.reshape(nblocks, blk, fw), w_first, b_first[None, :], w_second.T, tiles, tile_src.T,
         pair_count, send_blocks[0].T, labels.reshape(nblocks, blk),
     )
+    grad_first, grad_bias, grad_second = pl.pallas_call(
+        hand_over,
+        out_shape=tuple(jax.ShapeDtypeStruct(x.shape, F32) for x in (grad_first, grad_bias, grad_second)),
+        in_specs=[vm, vm, vm],
+        out_specs=(vm, vm, vm),
+    )(grad_first, grad_bias, grad_second)
     return (grad_first, grad_bias[0], grad_second.T)
 
 

time: 102 us -> 99.1 us (0.972)
  local copies, waits for them, and re-layouts: 4.11 us -> 0 us
  Pallas kernels: 97 us -> 98.1 us
    unnamed x3 -> x0, local copies, waits for them, and re-layouts: 4.11 us -> none
    pallas_call x0 -> x1, Pallas kernels: none -> 1.58 us  [shards(): pl.pallas_call(hand_over, out_shape=tuple((jax.ShapeDtypeStruct(x.shape,...]
where the time goes in v5:
time: 99.1 us; the launch traced here: 98.8 us
  Pallas kernels  98.1 us (99%)
    pallas_call x1, Pallas kernels, shards(): pl.pallas_call(functools.partial(whole_kernel, dims), out_shape=(jax.Shap...  96.6 us

profile of v5, /device:TPU:0, one launch (start us, length us, event | category | flops | bytes accessed | tf_op | source)
XLA Modules:
  0.0 98.8 jit_solution(13276782404127689446)
XLA Ops:
  0.6 96.6 %shard_map.112 = (f32[256,128]{1,0:T(8,128)}, f32[1,256]{1,0:T(1,128)}, f32[16,256]{1,0:T(8,128)}) custom-call(bf16[32,128,256]{2,1,0:T(8,128)(2,1)} %bitcast.10, bf16[256,1024]{1,0:T(8,128)(2,1)} %w_hbm.1, f32[1,256]{1,0:T(1,128)} %bitcast.15, bf16[16,256]{1,0:T(8,128)(2,1)} %bitcast.13, bf16[32,4,128,128]{3,2,1,0:T(8,128)(2,1)} %tiles.1, ...), custom_call_target="tpu_custom_call" | custom-call | flops 4294967296 | bytes 6291456 | tf_op jit(solution)/shard_map/pallas_call | solution.py:459
  97.2 1.6 %shard_map.113 = (f32[256,128]{1,0:T(8,128)}, f32[1,256]{1,0:T(1,128)}, f32[16,256]{1,0:T(8,128)}) custom-call(f32[256,128]{1,0:T(8,128)} %get-tuple-element.9.a, f32[1,256]{1,0:T(1,128)} %get-tuple-element.10.b, f32[16,256]{1,0:T(8,128)} %get-tuple-element.11.c), custom_call_target="tpu_custom_call" | custom-call | tf_op jit(solution)/shard_map/pallas_call | solution.py:529

commit v6 on v5

--- a/solution.py
+++ b/solution.py
@@ -133,13 +133,12 @@
     frecv_b[me_n] = fsend[1, me_n]
     second = []
     for d in range(1, parts):
-        first[d - 1].wait_send()
         x = exchange(1, d)
         x.start()
         second.append(x)
     fetch.wait()
     for x in first:
-        x.wait_recv()
+        x.wait()
 
     order = list(range(fsize - 1, -1, -1))
 

time: 99.1 us -> 99.1 us (level)
  no operation moved by 1% of the time
where the time goes in v6:
time: 99.1 us; the launch traced here: 98.9 us
  Pallas kernels  98.2 us (99%)
    pallas_call x1, Pallas kernels, shards(): pl.pallas_call(functools.partial(whole_kernel, dims), out_shape=(jax.Shap...  96.6 us

profile of v6, /device:TPU:0, one launch (start us, length us, event | category | flops | bytes accessed | tf_op | source)
XLA Modules:
  0.0 98.9 jit_solution(16326953051001204992)
XLA Ops:
  0.6 96.6 %shard_map.112 = (f32[256,128]{1,0:T(8,128)}, f32[1,256]{1,0:T(1,128)}, f32[16,256]{1,0:T(8,128)}) custom-call(bf16[32,128,256]{2,1,0:T(8,128)(2,1)} %bitcast.10, bf16[256,1024]{1,0:T(8,128)(2,1)} %w_hbm.1, f32[1,256]{1,0:T(1,128)} %bitcast.15, bf16[16,256]{1,0:T(8,128)(2,1)} %bitcast.13, bf16[32,4,128,128]{3,2,1,0:T(8,128)(2,1)} %tiles.1, ...), custom_call_target="tpu_custom_call" | custom-call | flops 4294967296 | bytes 6291456 | tf_op jit(solution)/shard_map/pallas_call | solution.py:458
  97.3 1.6 %shard_map.113 = (f32[256,128]{1,0:T(8,128)}, f32[1,256]{1,0:T(1,128)}, f32[16,256]{1,0:T(8,128)}) custom-call(f32[256,128]{1,0:T(8,128)} %get-tuple-element.9.a, f32[1,256]{1,0:T(1,128)} %get-tuple-element.10.b, f32[16,256]{1,0:T(8,128)} %get-tuple-element.11.c), custom_call_target="tpu_custom_call" | custom-call | tf_op jit(solution)/shard_map/pallas_call | solution.py:528
